TPU v7x, 32 devices: a whole 2x2x4 slice. The times are simulated.
32 devices in a mesh: elem: 8 (over y, x, core), four: 4 (over z).
Axes of the slice: x: 2, y: 2, z: 4, core: 2. Of those that a mesh axis runs over, the one named last changes fastest.
Arguments:
- adjoint_velocity: float32 [3, 2, 11, 360448], P(None, None, None, ('elem', 'four')), may hold values from -6 to 6
- base_flow: bfloat16 [3, 2, 11, 360448], P(None, None, None, ('elem', 'four')), may hold values from -6 to 6
- column_widths: float32 [128], P('elem'), may hold values from 0.03 to 0.65
- row_heights: float32 [2], replicated, may hold values from 0.06 to 0.18
- base_phase: int32 [1], replicated, may hold values from 0 to 255
Outputs:
- adjoint_next: float32 [3, 2, 11, 360448], P(None, None, None, ('elem', 'four'))
All inputs are finite; a program needn't handle non-finite values.
Results may differ from a plain program's by a relative error of at most 0.0003.
Values sent between devices are 32-bit elements; how exact they have to be, the bound alone decides.
A program may use at most 128 MiB of HBM per device.

v0:
```python
import jax
import jax.numpy as jnp
import numpy as np
from jax import lax
from jax.sharding import PartitionSpec as P

ITERS = 3


NU = 0.005
DT = 0.01
SIGMA = 1.0 / (NU * DT)
HIGHEST = lax.Precision.HIGHEST


def padded(x, sides, width):
    for axis, dim in sides:
        count, length = (lax.axis_size(axis), x.shape[dim])
        up = [(i, (i + 1) % count) for i in range(count - 1)]
        down = [(j, i) for i, j in up]
        last = lax.slice_in_dim(x, length - width, length, axis=dim)
        first = lax.slice_in_dim(x, 0, width, axis=dim)
        before = lax.ppermute(last, axis, up)
        after = lax.ppermute(first, axis, down)
        x = jnp.concatenate([before, x, after], axis=dim)
    return x


def legendre_values(points, node_count):
    table_rows = np.zeros((points.shape[0], node_count))
    table_rows[:, 0] = 1.0
    table_rows[:, 1] = points
    for degree_now in range(2, node_count):
        table_rows[:, degree_now] = (
            (2 * degree_now - 1) * points * table_rows[:, degree_now - 1]
            - (degree_now - 1) * table_rows[:, degree_now - 2]
        ) / degree_now
    return table_rows


def gll_tables(node_count):
    degree = node_count - 1
    points = np.cos(np.pi * np.arange(node_count) / degree)
    for newton_step in range(60):
        legendre = legendre_values(points, node_count)
        points = points - (points * legendre[:, degree] - legendre[:, degree - 1]) / (
            node_count * legendre[:, degree]
        )
    legendre = legendre_values(points, node_count)
    weights = 2.0 / (degree * node_count * legendre[:, degree] ** 2)
    points = points[::-1]
    weights = weights[::-1]
    end_values = legendre[::-1, degree]
    derivative = np.zeros((node_count, node_count))
    for row_index in range(node_count):
        for column in range(node_count):
            if row_index != column:
                derivative[row_index, column] = end_values[row_index] / (
                    end_values[column] * (points[row_index] - points[column])
                )
    derivative[0, 0] = -degree * node_count / 4.0
    derivative[degree, degree] = degree * node_count / 4.0
    return (jnp.asarray(derivative.astype(np.float32)), jnp.asarray(weights.astype(np.float32)))


def fourier_table(plane_count):
    positions = np.arange(plane_count)
    basis_rows = np.zeros((plane_count, plane_count))
    basis_rows[0] = 1.0 / np.sqrt(plane_count)
    basis_rows[1] = np.cos(np.pi * positions) / np.sqrt(plane_count)
    for wave_index in range(1, plane_count // 2):
        basis_rows[2 * wave_index] = np.sqrt(2.0 / plane_count) * np.cos(
            2.0 * np.pi * wave_index * positions / plane_count
        )
        basis_rows[2 * wave_index + 1] = np.sqrt(2.0 / plane_count) * np.sin(
            2.0 * np.pi * wave_index * positions / plane_count
        )
    wave_counts = np.arange(plane_count) // 2
    wave_counts[1] = plane_count // 2
    wave_counts[0] = 0
    wavenumbers = 2.0 * np.pi * wave_counts / (plane_count / 64.0)
    rotate = np.zeros((plane_count, plane_count))
    for wave_index in range(1, plane_count // 2):
        rotate[2 * wave_index, 2 * wave_index + 1] = wavenumbers[2 * wave_index]
        rotate[2 * wave_index + 1, 2 * wave_index] = -wavenumbers[2 * wave_index]
    span_slope = basis_rows.T @ rotate @ basis_rows
    return (
        jnp.asarray(basis_rows.astype(np.float32)),
        jnp.asarray(wavenumbers.astype(np.float32)),
        jnp.asarray(span_slope.astype(np.float32)),
    )


def slope_height(values, heights, derivative):
    turned = jnp.einsum("km,...ympx->...ykpx", derivative, values, precision=HIGHEST)
    return turned * (2.0 / heights).reshape(-1, 1, 1, 1)


def line_slope_width(values, widths, derivative):
    node_count = derivative.shape[0]
    shaped = values.reshape(values.shape[:-2] + (widths.shape[0], node_count, values.shape[-1]))
    turned = jnp.einsum("km,...cmz->...ckz", derivative, shaped, precision=HIGHEST)
    return (turned * (2.0 / widths)[:, None, None]).reshape(values.shape)


def line_slope_span(values, span_slope):
    return jnp.einsum("zw,...w->...z", span_slope, values, precision=HIGHEST)


def line_gradients(values, widths, heights, derivative, span_slope):
    return (
        line_slope_width(values, widths, derivative),
        slope_height(values, heights, derivative),
        line_slope_span(values, span_slope),
    )


def advect(line_values, slopes, base_now, base_slopes):
    pieces = []
    for component in range(3):
        summed = (
            base_now[0] * slopes[0][component]
            + base_now[1] * slopes[1][component]
            + base_now[2] * slopes[2][component]
        )
        summed = summed - (
            line_values[0] * base_slopes[component][0]
            + line_values[1] * base_slopes[component][1]
            + line_values[2] * base_slopes[component][2]
        )
        pieces.append(summed)
    return jnp.stack(pieces)


def assemble_rows(joined, node_count):
    first_row = joined[..., :, 0, :, :]
    last_row = joined[..., :, node_count - 1, :, :]
    shared = last_row[..., :-1, :, :] + first_row[..., 1:, :, :]
    new_first = jnp.concatenate([first_row[..., :1, :, :], shared], axis=-3)
    new_last = jnp.concatenate([shared, last_row[..., -1:, :, :]], axis=-3)
    return jnp.concatenate(
        [
            new_first[..., :, None, :, :],
            joined[..., :, 1 : node_count - 1, :, :],
            new_last[..., :, None, :, :],
        ],
        axis=-3,
    )


def edge_assemble(values, is_first, is_last, node_count):
    extended = padded(values, (("elem", 4),), 1)
    following = extended[..., 2:]
    preceding = extended[..., :-2]
    joined = values + jnp.where(is_last, following, 0.0) + jnp.where(is_first, preceding, 0.0)
    return assemble_rows(joined, node_count)


def inner_product(left, right, weight):
    return jnp.sum(left * right * weight, axis=(-4, -3, -1), keepdims=True)


def paired_products(residual, image_vec, weight):
    return lax.psum(
        (inner_product(residual, residual, weight), inner_product(residual, image_vec, weight)),
        "elem",
    )


def local(adjoint_velocity, base_flow, column_widths, row_heights, base_phase):
    node_count = adjoint_velocity.shape[2]
    row_count = adjoint_velocity.shape[1]
    columns_here = column_widths.shape[0]
    part_nodes = columns_here * node_count
    planes_local = adjoint_velocity.shape[3] // part_nodes
    adjoint_local = adjoint_velocity.reshape(3, row_count, node_count, planes_local, part_nodes)
    plane_parts = lax.axis_size("four")
    plane_total = planes_local * plane_parts
    columns_line = columns_here // plane_parts
    line_nodes = columns_line * node_count
    base_local = base_flow.reshape(3, row_count, node_count, line_nodes, plane_total)
    basis_rows, wavenumbers, span_slope = fourier_table(plane_total)
    derivative, weights = gll_tables(node_count)
    wave_local = lax.dynamic_slice_in_dim(
        wavenumbers, lax.axis_index("four") * planes_local, planes_local
    )
    line_widths = lax.dynamic_slice_in_dim(
        column_widths, lax.axis_index("four") * columns_line, columns_line
    )
    node_widths = jnp.repeat(column_widths, node_count)
    node_weights = jnp.tile(weights, columns_here)
    eye_cols = jnp.eye(columns_here, dtype=jnp.float32)
    block_turn = jnp.kron(eye_cols, derivative.T)
    block_back = jnp.kron(eye_cols, derivative)
    base_now = jnp.roll(base_local.astype(jnp.float32), base_phase[0], axis=4)
    base_slopes = line_gradients(base_now, line_widths, row_heights, derivative, span_slope)
    sending = jnp.transpose(adjoint_local, (0, 1, 2, 4, 3))
    arrived = lax.all_to_all(sending, "four", split_axis=3, concat_axis=4, tiled=True)
    line_values = jnp.einsum("jz,...xj->...xz", basis_rows, arrived, precision=HIGHEST)
    slopes = line_gradients(line_values, line_widths, row_heights, derivative, span_slope)
    advection = advect(line_values, slopes, base_now, base_slopes)
    advection_hat = jnp.einsum("jz,...xz->...xj", basis_rows, advection, precision=HIGHEST)
    returned = lax.all_to_all(advection_hat, "four", split_axis=4, concat_axis=3, tiled=True)
    returned = jnp.transpose(returned, (0, 1, 2, 4, 3))
    node_x = jnp.arange(part_nodes, dtype=jnp.int32)
    place_x = node_x % node_count
    is_first = place_x == 0
    is_last = place_x == node_count - 1
    height_b = row_heights.reshape(-1, 1, 1, 1)
    weight_y = weights.reshape(-1, 1, 1)
    source = SIGMA * adjoint_local + returned / NU
    local_side = node_widths * height_b * 0.25 * weight_y * node_weights * source
    right_side = edge_assemble(local_side, is_first, is_last, node_count)
    column_x = lax.axis_index("elem") * columns_here + node_x // node_count
    last_column = columns_here * lax.axis_size("elem") - 1
    shared_x = is_first & (column_x > 0) | is_last & (column_x < last_column)
    node_y = jnp.arange(row_count * node_count, dtype=jnp.int32)
    place_y = node_y % node_count
    row_y = node_y // node_count
    shared_y = (place_y == 0) & (row_y > 0) | (place_y == node_count - 1) & (row_y < row_count - 1)
    mult_x = 1.0 + shared_x.astype(jnp.float32)
    mult_y = 1.0 + shared_y.astype(jnp.float32)
    weight = (1.0 / (mult_y[:, None] * mult_x[None, :])).reshape(
        row_count, node_count, 1, part_nodes
    )
    wave_b = (wave_local * wave_local).reshape(-1, 1)

    def helmholtz(values):
        along_x = jnp.einsum("...n,nm->...m", values, block_turn, precision=HIGHEST) * node_weights
        back_x = jnp.einsum("...n,nm->...m", along_x, block_back, precision=HIGHEST)
        along_y = (
            jnp.einsum("km,...ympx->...ykpx", derivative, values, precision=HIGHEST) * weight_y
        )
        back_y = jnp.einsum("km,...ykpx->...ympx", derivative, along_y, precision=HIGHEST)
        summed = (
            height_b / node_widths * weight_y * back_x
            + node_widths / height_b * node_weights * back_y
        )
        summed = (
            summed
            + (wave_b + SIGMA) * (node_widths * height_b * 0.25) * weight_y * node_weights * values
        )
        return edge_assemble(summed, is_first, is_last, node_count)

    solution = jnp.zeros_like(right_side)
    residual = right_side
    image_vec = helmholtz(residual)
    norm_now, product = paired_products(residual, image_vec, weight)
    step_size = norm_now / product
    direction = residual
    along = image_vec
    for iteration in range(ITERS):
        solution = solution + step_size * direction
        residual = residual - step_size * along
        if iteration + 1 < ITERS:
            image_vec = helmholtz(residual)
            norm_next, product = paired_products(residual, image_vec, weight)
            growth = norm_next / norm_now
            step_size = norm_next / (product - growth * norm_next / step_size)
            direction = residual + growth * direction
            along = image_vec + growth * along
            norm_now = norm_next
    return solution.reshape(3, row_count, node_count, planes_local * part_nodes)


def solution(mesh):
    return jax.shard_map(
        local,
        mesh=mesh,
        in_specs=(
            P(None, None, None, ("elem", "four")),
            P(None, None, None, ("elem", "four")),
            P("elem"),
            P(),
            P(),
        ),
        out_specs=P(None, None, None, ("elem", "four")),
        check_vma=False,
    )
```

profile of v0, /device:TPU:25, one launch (start us, length us, event | category | flops | bytes accessed | tf_op | source)
XLA Modules:
  0.0 654.6 jit_solution(6182444263756402957)
XLA Ops:
  2.0 6.1 reshape.292
  8.2 9.3 %copy.291 = f32[3,2,11,176,64]{4,1,0,2,3:T(2,128)} copy(f32[3,2,11,176,64]{3,4,1,0,2:T(8,128)} %bitcast.209) | data formatting | bytes 5947392 | tf_op jit(solution)/shard_map/transpose | solution.py:197
  17.5 8.6 %reshape.308 = f32[4,1,185856]{2,1,0:T(1,128)} reshape(f32[176,11,3,2,64]{4,3,2,1,0:T(2,128)} %bitcast.212) | data formatting | bytes 5947392
  26.1 4.7 all-to-all-start
  55.2 39.7 %all-to-all-done = f32[4,1,185856]{2,1,0:T(1,128)} async-done(((f32[4,1,185856]{2,1,0:T(1,128)}), f32[4,1,185856]{2,1,0:T(1,128)}, u32[]{:S(2)}, u32[]{:S(2)}) %all-to-all-start) | async-done | bytes 2973728 | tf_op jit(solution)/shard_map/all_to_all | solution.py:198
  95.4 11.3 %reduce = f32[4,185856]{1,0:T(4,128)} reduce(f32[4,1,185856]{2,1,0:T(1,128)} %all-to-all-done, f32[]{:T(128)} %broadcast.352), dimensions={1}, to_apply=%all_to_all.20.reduce_sub_computation | reduce | bytes 5947396 | tf_op jit(solution)/shard_map/all_to_all | solution.py:198
  106.7 9.1 %reshape.309 = f32[176,11,3,2,64]{4,3,2,1,0:T(2,128)} reshape(f32[4,185856]{1,0:T(4,128)} %reduce) | data formatting | bytes 5947392
  115.8 6.7 %copy.385 = f32[3,2,11,44,4,64]{5,4,3,2,1,0:T(4,128)} copy(f32[3,2,11,44,4,64]{5,1,0,2,3,4:T(2,128)} %bitcast.213) | data formatting | bytes 5947392 | tf_op jit(solution)/shard_map/all_to_all | solution.py:198
  122.5 6.7 %reshape.304 = f32[3,2,11,44,256]{4,3,2,1,0:T(8,128)} reshape(f32[3,2,11,44,4,64]{5,4,3,2,1,0:T(4,128)} %copy.385) | data formatting | bytes 5947392 | tf_op jit(solution)/shard_map/all_to_all | solution.py:198
  129.2 4.7 convolution_bitcast_fusion
  136.6 6.1 fusion.43
  155.8 6.0 fusion.53
  170.8 10.2 %copy.315 = f32[3,2,11,44,256]{3,1,2,0,4:T(2,128)} copy(f32[3,2,11,44,256]{4,3,2,1,0:T(8,128)S(1)} %fusion.47) | data formatting | bytes 5947392 | tf_op jit(solution)/shard_map/jz,...xz->...xj/dot_general | solution.py:202
  180.9 19.5 %reshape.310 = f32[4,1,185856]{2,1,0:T(1,128)} reshape(f32[256,3,11,2,44]{4,3,2,1,0:T(2,128)} %bitcast.211) | data formatting | bytes 5947392
  200.5 7.2 %all-to-all-start.1 = ((f32[4,1,185856]{2,1,0:T(1,128)}), f32[4,1,185856]{2,1,0:T(1,128)}, u32[]{:S(2)}, u32[]{:S(2)}) async-start(f32[4,1,185856]{2,1,0:T(1,128)} %reshape.310), calls=%async_computation.1 | async-start | bytes 5947392 | tf_op jit(solution)/shard_map/all_to_all | solution.py:203
  210.0 61.2 %all-to-all-done.1 = f32[4,1,185856]{2,1,0:T(1,128)} async-done(((f32[4,1,185856]{2,1,0:T(1,128)}), f32[4,1,185856]{2,1,0:T(1,128)}, u32[]{:S(2)}, u32[]{:S(2)}) %all-to-all-start.1) | async-done | bytes 2973728 | tf_op jit(solution)/shard_map/all_to_all | solution.py:203
  271.2 11.5 %reduce.1 = f32[4,185856]{1,0:T(4,128)} reduce(f32[4,1,185856]{2,1,0:T(1,128)} %all-to-all-done.1, f32[]{:T(128)} %broadcast.352), dimensions={1}, to_apply=%all_to_all.24.reduce_sub_computation | reduce | bytes 5947396 | tf_op jit(solution)/shard_map/all_to_all | solution.py:203
  282.7 20.9 %reshape.311 = f32[256,3,11,2,44]{4,3,2,1,0:T(2,128)} reshape(f32[4,185856]{1,0:T(4,128)} %reduce.1) | data formatting | bytes 5947392
  303.7 13.5 %copy.316 = f32[3,2,11,44,256]{4,1,3,2,0:T(2,128)} copy(f32[3,2,11,44,256]{3,1,2,0,4:T(2,128)} %bitcast.210) | data formatting | bytes 5947392 | tf_op jit(solution)/shard_map/all_to_all | solution.py:203
  317.2 4.7 broadcast_multiply_fusion
  321.9 7.6 %div.134 = f32[3,2,11,44,4,64]{5,4,1,3,2,0:T(4,128)} reshape(f32[3,2,11,44,256]{4,1,3,2,0:T(2,128)} %broadcast_multiply_fusion) | data formatting | bytes 5947392 | tf_op jit(solution)/shard_map/div | solution.py:211
  329.5 8.3 %copy.317 = f32[3,2,11,4,44,64]{5,1,4,3,2,0:T(2,128)} copy(f32[3,2,11,4,44,64]{5,3,1,4,2,0:T(4,128)} %bitcast.214) | data formatting | bytes 5947392 | tf_op jit(solution)/shard_map/div | solution.py:211
  337.8 9.5 %copy.318 = f32[3,2,11,176,64]{3,4,1,0,2:T(8,128)} copy(f32[3,2,11,176,64]{4,1,3,2,0:T(2,128)} %bitcast.215) | data formatting | bytes 5947392 | tf_op jit(solution)/shard_map/div | solution.py:211
  347.3 4.5 fusion.34
  357.8 5.4 collective-permute-start.1
  374.3 8.0 %fusion.28 = f32[3,2,11,64,176]{4,3,1,0,2:T(8,128)S(1)} fusion(f32[3,2,11,64,176]{4,3,1,0,2:T(8,128)} %copy-done.6, f32[3,2,11,64,1]{4,3,1,0,2:T(8,128)} %copy.322, f32[3,2,11,64,1]{4,3,1,0,2:T(8,128)} %copy.320, pred[176]{0:T(512)(128)(4,1)S(1)} %get-tuple-element.88, pred[176]{0:T(512)(128)(4,1)S(1)} %get-tuple-element.87), kind=kLoop, calls=%fused_computation.35 | loop fusion | flops 4460544 | bytes 5981536 | tf_op jit(solution)/shard_map/add | solution.py:155
  384.4 9.2 %fusion.10 = f32[3,2,64,176,11]{3,4,2,1,0:T(8,128)S(1)} fusion(f32[11,11,1,1,1]{1,0,4,3,2:T(8,128)S(1)} %copy-done.31, f32[3,2,11,64,176]{4,3,2,1,0:T(8,128)S(1)} %pad_maximum_fusion.8), kind=kOutput, calls=%fused_computation.10 | convolution fusion | flops 98131968 | bytes 5947876 | tf_op jit(solution)/shard_map/km,...ympx->...ykpx/dot_general | solution.py:232
  393.7 7.9 %fusion.4 = f32[3,2,64,176,11]{3,4,2,1,0:T(8,128)S(1)} fusion(f32[11,11,1,1,1]{1,0,4,3,2:T(8,128)S(1)} %copy-done.31, f32[3,2,64,176,11]{3,4,2,1,0:T(8,128)S(1)} %fusion.10, f32[11]{0:T(128)S(1)} %copy-done.35), kind=kOutput, calls=%fused_computation.4 | convolution fusion | flops 98875392 | bytes 5947920 | tf_op jit(solution)/shard_map/km,...ykpx->...ympx/dot_general | solution.py:234
  405.3 6.4 fusion.33
  430.7 7.9 %fusion.24 = f32[3,2,11,64,176]{4,3,1,0,2:T(8,128)S(1)} fusion(f32[3,2,11,64,176]{4,3,1,0,2:T(8,128)} %copy-done.7, f32[3,2,11,64,1]{4,3,1,0,2:T(8,128)} %copy.334, f32[3,2,11,64,1]{4,3,1,0,2:T(8,128)} %copy.332, pred[176]{0:T(512)(128)(4,1)S(1)} %get-tuple-element.88, pred[176]{0:T(512)(128)(4,1)S(1)} %get-tuple-element.87), kind=kLoop, calls=%fused_computation.29 | loop fusion | flops 4460544 | bytes 5981536 | tf_op jit(solution)/shard_map/add | solution.py:155
  442.1 11.5 %all-reduce.2 = (f32[3,1,1,64,1]{3,0,4,2,1:T(4,128)S(1)}, f32[3,1,1,64,1]{3,0,4,2,1:T(4,128)S(1)}) all-reduce(f32[3,1,1,64,1]{3,0,4,2,1:T(4,128)} %bitcast.234, f32[3,1,1,64,1]{3,0,4,2,1:T(4,128)} %bitcast.233), channel_id=1, replica_groups=mesh['elem'=8,'four'=4] {'elem'}, use_global_device_ids=true, to_apply=%region_1.2 | all-reduce | flops 384 | bytes 3072 | tf_op jit(solution)/shard_map/psum | solution.py:164
  457.6 9.2 %fusion.8 = f32[3,2,64,176,11]{3,4,2,1,0:T(8,128)S(1)} fusion(f32[11,11,1,1,1]{1,0,4,3,2:T(8,128)S(1)} %copy-done.31, f32[3,2,11,64,176]{4,3,2,1,0:T(8,128)S(1)} %multiply_subtract_fusion.1), kind=kOutput, calls=%fused_computation.8 | convolution fusion | flops 98131968 | bytes 5947876 | tf_op jit(solution)/shard_map/km,...ympx->...ykpx/dot_general | solution.py:232
  470.7 7.4 %fusion.2 = f32[3,2,64,176,11]{3,4,2,1,0:T(8,128)S(1)} fusion(f32[11,11,1,1,1]{1,0,4,3,2:T(8,128)S(1)} %copy-done.31, f32[3,2,64,176,11]{3,4,2,1,0:T(8,128)S(1)} %fusion.8, f32[11]{0:T(128)S(1)} %copy-done.35), kind=kOutput, calls=%fused_computation.2 | convolution fusion | flops 98875392 | bytes 5947920 | tf_op jit(solution)/shard_map/km,...ykpx->...ympx/dot_general | solution.py:234
  478.1 6.4 fusion.32
  490.3 4.3 collective-permute-start.5
  504.2 7.8 %fusion.20 = f32[3,2,11,64,176]{4,3,1,0,2:T(8,128)S(1)} fusion(f32[3,2,11,64,176]{4,3,1,0,2:T(8,128)} %copy-done.8, f32[3,2,11,64,1]{4,3,1,0,2:T(8,128)} %copy.348, f32[3,2,11,64,1]{4,3,1,0,2:T(8,128)} %copy.346, pred[176]{0:T(512)(128)(4,1)S(1)} %copy-done.52, pred[176]{0:T(512)(128)(4,1)S(1)} %copy-done.49), kind=kLoop, calls=%fused_computation.23 | loop fusion | flops 4460544 | bytes 5981536 | tf_op jit(solution)/shard_map/add | solution.py:155
  515.4 13.1 %all-reduce.1 = (f32[3,1,1,64,1]{3,0,4,2,1:T(4,128)S(1)}, f32[3,1,1,64,1]{3,0,4,2,1:T(4,128)S(1)}) all-reduce(f32[3,1,1,64,1]{3,0,4,2,1:T(4,128)} %bitcast.236, f32[3,1,1,64,1]{3,0,4,2,1:T(4,128)} %bitcast.235), channel_id=1, replica_groups=mesh['elem'=8,'four'=4] {'elem'}, use_global_device_ids=true, to_apply=%region_5.6 | all-reduce | flops 384 | bytes 3072 | tf_op jit(solution)/shard_map/psum | solution.py:164
  529.8 5.4 multiply_subtract_fusion
  535.3 9.2 %fusion.6 = f32[3,2,64,176,11]{3,4,2,1,0:T(8,128)S(1)} fusion(f32[11,11,1,1,1]{1,0,4,3,2:T(8,128)S(1)} %copy-done.31, f32[3,2,11,64,176]{4,3,2,1,0:T(8,128)S(1)} %multiply_subtract_fusion), kind=kOutput, calls=%fused_computation.6 | convolution fusion | flops 98131968 | bytes 5947876 | tf_op jit(solution)/shard_map/km,...ympx->...ykpx/dot_general | solution.py:232
  548.4 7.4 %fusion = f32[3,2,64,176,11]{3,4,2,1,0:T(8,128)S(1)} fusion(f32[11,11,1,1,1]{1,0,4,3,2:T(8,128)S(1)} %copy-done.31, f32[3,2,64,176,11]{3,4,2,1,0:T(8,128)S(1)} %fusion.6, f32[11]{0:T(128)S(1)} %copy-done.35), kind=kOutput, calls=%fused_computation | convolution fusion | flops 98875392 | bytes 5947920 | tf_op jit(solution)/shard_map/km,...ykpx->...ympx/dot_general | solution.py:234
  555.8 6.4 fusion.31
  567.9 4.2 collective-permute-start.7
  579.8 4.3 concatenate.111
  591.1 4.3 reshape.307
  605.0 4.4 concatenate.129
  613.6 7.2 %fusion.16 = f32[3,2,11,64,176]{4,3,1,0,2:T(8,128)S(1)} fusion(f32[3,2,11,64,176]{4,3,1,0,2:T(8,128)} %copy-done.5, f32[3,2,11,64,1]{4,3,1,0,2:T(8,128)S(1)} %copy.363, f32[3,2,11,64,1]{4,3,1,0,2:T(8,128)} %copy.361, pred[176]{0:T(512)(128)(4,1)S(1)} %copy-done.53, pred[176]{0:T(512)(128)(4,1)S(1)} %copy-done.50), kind=kLoop, calls=%fused_computation.17 | loop fusion | flops 4460544 | bytes 5981536 | tf_op jit(solution)/shard_map/add | solution.py:155
  624.5 12.5 %all-reduce = (f32[3,1,1,64,1]{3,0,4,2,1:T(4,128)S(1)}, f32[3,1,1,64,1]{3,0,4,2,1:T(4,128)S(1)}) all-reduce(f32[3,1,1,64,1]{3,0,4,2,1:T(4,128)S(1)} %bitcast.232, f32[3,1,1,64,1]{3,0,4,2,1:T(4,128)S(1)} %bitcast.231), channel_id=1, replica_groups=mesh['elem'=8,'four'=4] {'elem'}, use_global_device_ids=true, to_apply=%region_9.10 | all-reduce | flops 384 | bytes 3072 | tf_op jit(solution)/shard_map/psum | solution.py:164
  642.2 12.2 %multiply_add_fusion = f32[3,2,11,11264]{3,1,2,0:T(2,128)} fusion(f32[3,2,1,11264]{3,1,2,0:T(2,128)} %bitcast.229, f32[3,2,1,11264]{3,1,2,0:T(2,128)} %bitcast.230, f32[3,2,1,11264]{3,1,2,0:T(2,128)S(1)} %bitcast.227, f32[3,2,1,11264]{3,1,2,0:T(2,128)S(1)} %bitcast.228, f32[3,2,1,11264]{3,1,2,0:T(2,128)S(1)} %bitcast.225, ...), kind=kLoop, calls=%fused_computation.99 | loop fusion | flops 15611904 | bytes 12570624 | tf_op jit(solution)/shard_map/add | solution.py:253
  (267 shorter events, 172.8 us)
Async XLA Ops:
  26.1 68.8 %all-to-all-start = ((f32[4,1,185856]{2,1,0:T(1,128)}), f32[4,1,185856]{2,1,0:T(1,128)}, u32[]{:S(2)}, u32[]{:S(2)}) async-start(f32[4,1,185856]{2,1,0:T(1,128)} %reshape.308), calls=%async_computation | async-start | bytes 5947392 | tf_op jit(solution)/shard_map/all_to_all | solution.py:198
  122.5 6.7 %copy-start.26 = (f32[256,256,1,1,1]{1,0,4,3,2:T(8,128)S(1)}, f32[256,256,1,1,1]{1,0,4,3,2:T(8,128)}, u32[]{:S(2)}) copy-start(f32[256,256,1,1,1]{1,0,4,3,2:T(8,128)} %constant.113) | copy-start | bytes 786436
  145.5 10.3 %slice-start.9 = ((s8[4325376]{0:T(1024)(128)(4,1)}), s8[4194304]{0:T(1024)(128)(4,1)S(1)}, s32[]{:S(2)}) async-start(s8[4325376]{0:T(1024)(128)(4,1)} %bitcast.216), calls=%async_computation.11 | async-start | bytes 8388608
  149.6 6.2 slice-start.10
  155.8 6.0 copy-start.11
  200.5 7.4 %copy-start.35 = (f32[11]{0:T(128)S(1)}, f32[11]{0:T(128)}, u32[]{:S(2)}) copy-start(f32[11]{0:T(128)} %constant.111.clone) | copy-start | bytes 136
  200.5 7.5 %copy-start.61 = (f32[256]{0:T(256)S(1)}, f32[256]{0:T(256)}, u32[]{:S(2)}) copy-start(f32[256]{0:T(256)} %constant.108.clone) | copy-start | bytes 3076
  200.5 8.1 %copy-start.46 = (f32[11,11]{1,0:T(8,128)S(1)}, f32[11,11]{1,0:T(8,128)}, u32[]{:S(2)}) copy-start(f32[11,11]{1,0:T(8,128)} %constant.110.clone) | copy-start | bytes 1456
  200.5 8.1 %copy-start.47 = (f32[11,11]{1,0:T(8,128)S(1)}, f32[11,11]{1,0:T(8,128)}, u32[]{:S(2)}) copy-start(f32[11,11]{1,0:T(8,128)} %constant.112) | copy-start | bytes 1456
  200.5 70.7 %all-to-all-start.1 = ((f32[4,1,185856]{2,1,0:T(1,128)}), f32[4,1,185856]{2,1,0:T(1,128)}, u32[]{:S(2)}, u32[]{:S(2)}) async-start(f32[4,1,185856]{2,1,0:T(1,128)} %reshape.310), calls=%async_computation.1 | async-start | bytes 5947392 | tf_op jit(solution)/shard_map/all_to_all | solution.py:203
  208.0 222.6 %copy-start.48 = (pred[176]{0:T(512)(128)(4,1)}, pred[176]{0:T(512)(128)(4,1)S(1)}, u32[]{:S(2)}) copy-start(pred[176]{0:T(512)(128)(4,1)S(1)} %get-tuple-element.87) | copy-start | bytes 532
  208.1 222.6 %copy-start.51 = (pred[176]{0:T(512)(128)(4,1)}, pred[176]{0:T(512)(128)(4,1)S(1)}, u32[]{:S(2)}) copy-start(pred[176]{0:T(512)(128)(4,1)S(1)} %get-tuple-element.88) | copy-start | bytes 532
  208.1 197.1 %copy-start.36 = (f32[2,176]{1,0:T(2,128)}, f32[2,176]{1,0:T(2,128)S(1)}, u32[]{:S(2)}) copy-start(f32[2,176]{1,0:T(2,128)S(1)} %get-tuple-element.81) | copy-start | bytes 4228
  208.2 197.0 %copy-start.32 = (f32[2,11,176]{2,0,1:T(2,128)}, f32[2,11,176]{2,0,1:T(2,128)S(1)}, u32[]{:S(2)}) copy-start(f32[2,11,176]{2,0,1:T(2,128)S(1)} %get-tuple-element.83) | copy-start | bytes 46468
  357.8 12.4 %collective-permute-start.1 = (f32[3,2,11,64,1]{3,1,4,2,0:T(2,128)S(1)}, f32[3,2,11,64,1]{3,1,4,2,0:T(2,128)S(1)}, u32[]{:S(2)}, u32[]{:S(2)}) collective-permute-start(f32[3,2,11,64,1]{3,1,4,2,0:T(2,128)S(1)} %copy.321), channel_id=1, source_target_pairs={{0,4},{4,8},{8,12},{12,16},{16,20},{20,24},{24,28},{1,5},{5,9},{9,... | collective-permute-start | bytes 50696 | tf_op jit(solution)/shard_map/ppermute | solution.py:23
  365.5 6.7 %collective-permute-start = (f32[3,2,11,64,1]{3,1,4,2,0:T(2,128)S(1)}, f32[3,2,11,64,1]{3,1,4,2,0:T(2,128)S(1)}, u32[]{:S(2)}, u32[]{:S(2)}) collective-permute-start(f32[3,2,11,64,1]{3,1,4,2,0:T(2,128)S(1)} %copy.319), channel_id=1, source_target_pairs={{4,0},{8,4},{12,8},{16,12},{20,16},{24,20},{28,24},{5,1},{9,5},{13... | collective-permute-start | bytes 50696 | tf_op jit(solution)/shard_map/ppermute | solution.py:24
  382.3 19.2 %copy-start.2 = (f32[3,2,11,64,176]{4,3,1,0,2:T(8,128)}, f32[3,2,11,64,176]{4,3,1,0,2:T(8,128)S(1)}, u32[]{:S(2)}) copy-start(f32[3,2,11,64,176]{4,3,1,0,2:T(8,128)S(1)} %fusion.28) | copy-start | bytes 8921092
  417.4 8.0 %collective-permute-start.3 = (f32[3,2,11,64,1]{3,1,4,2,0:T(2,128)S(1)}, f32[3,2,11,64,1]{3,1,4,2,0:T(2,128)S(1)}, u32[]{:S(2)}, u32[]{:S(2)}) collective-permute-start(f32[3,2,11,64,1]{3,1,4,2,0:T(2,128)S(1)} %copy.333), channel_id=1, source_target_pairs={{0,4},{4,8},{8,12},{12,16},{16,20},{20,24},{24,28},{1,5},{5,9},{9,... | collective-permute-start | bytes 50696 | tf_op jit(solution)/shard_map/ppermute | solution.py:23
  423.4 5.2 collective-permute-start.2
  425.4 88.2 %copy-start.29 = (f32[2,11,176]{2,1,0:T(8,128)}, f32[2,11,176]{2,1,0:T(8,128)S(1)}, u32[]{:S(2)}) copy-start(f32[2,11,176]{2,1,0:T(8,128)S(1)} %multiply_divide_fusion) | copy-start | bytes 46468
  428.6 11.4 %slice-start.4 = ((s8[4325376]{0:T(1024)(128)(4,1)}), s8[131072]{0:T(1024)(128)(4,1)S(1)}, s32[]{:S(2)}) async-start(s8[4325376]{0:T(1024)(128)(4,1)} %bitcast.206), calls=%async_computation.6 | async-start | bytes 262144
  430.7 9.4 %slice-start.5 = ((s8[4325376]{0:T(1024)(128)(4,1)}), s8[4194304]{0:T(1024)(128)(4,1)S(1)}, s32[]{:S(2)}) async-start(s8[4325376]{0:T(1024)(128)(4,1)} %bitcast.206), calls=%async_computation.7 | async-start | bytes 8388608
  457.6 20.5 %copy-start = (f32[3,2,11,64,176]{4,3,2,1,0:T(8,128)}, f32[3,2,11,64,176]{4,3,2,1,0:T(8,128)S(1)}, u32[]{:S(2)}) copy-start(f32[3,2,11,64,176]{4,3,2,1,0:T(8,128)S(1)} %multiply_subtract_fusion.1) | copy-start | bytes 8921092
  470.7 7.4 %copy-start.33 = (f32[2,11,176]{2,0,1:T(2,128)S(1)}, f32[2,11,176]{2,0,1:T(2,128)}, u32[]{:S(2)}) copy-start(f32[2,11,176]{2,0,1:T(2,128)} %copy-done.32) | copy-start | bytes 46468
  470.7 7.4 %copy-start.37 = (f32[2,176]{1,0:T(2,128)S(1)}, f32[2,176]{1,0:T(2,128)}, u32[]{:S(2)}) copy-start(f32[2,176]{1,0:T(2,128)} %copy-done.36) | copy-start | bytes 4228
  490.3 14.0 %copy-start.49 = (pred[176]{0:T(512)(128)(4,1)S(1)}, pred[176]{0:T(512)(128)(4,1)}, u32[]{:S(2)}) copy-start(pred[176]{0:T(512)(128)(4,1)} %copy-done.48) | copy-start | bytes 532
  490.3 14.0 %copy-start.52 = (pred[176]{0:T(512)(128)(4,1)S(1)}, pred[176]{0:T(512)(128)(4,1)}, u32[]{:S(2)}) copy-start(pred[176]{0:T(512)(128)(4,1)} %copy-done.51) | copy-start | bytes 532
  490.3 8.6 %collective-permute-start.5 = (f32[3,2,11,64,1]{3,1,4,2,0:T(2,128)S(1)}, f32[3,2,11,64,1]{3,1,4,2,0:T(2,128)S(1)}, u32[]{:S(2)}, u32[]{:S(2)}) collective-permute-start(f32[3,2,11,64,1]{3,1,4,2,0:T(2,128)S(1)} %copy.347), channel_id=1, source_target_pairs={{0,4},{4,8},{8,12},{12,16},{16,20},{20,24},{24,28},{1,5},{5,9},{9,... | collective-permute-start | bytes 50696 | tf_op jit(solution)/shard_map/ppermute | solution.py:23
  496.9 5.2 collective-permute-start.4
  502.2 11.4 %slice-start = ((s8[4325376]{0:T(1024)(128)(4,1)}), s8[131072]{0:T(1024)(128)(4,1)S(1)}, s32[]{:S(2)}) async-start(s8[4325376]{0:T(1024)(128)(4,1)} %bitcast.202), calls=%async_computation.2 | async-start | bytes 262144
  504.2 9.3 %slice-start.1 = ((s8[4325376]{0:T(1024)(128)(4,1)}), s8[4194304]{0:T(1024)(128)(4,1)S(1)}, s32[]{:S(2)}) async-start(s8[4325376]{0:T(1024)(128)(4,1)} %bitcast.202), calls=%async_computation.3 | async-start | bytes 8388608
  528.6 6.7 %copy-start.56 = (f32[3,1,1,64,1]{3,0,4,2,1:T(4,128)}, f32[3,1,1,64,1]{3,0,4,2,1:T(4,128)S(1)}, u32[]{:S(2)}) copy-start(f32[3,1,1,64,1]{3,0,4,2,1:T(4,128)S(1)} %get-tuple-element.13) | copy-start | bytes 2308
  535.3 20.5 %copy-start.1 = (f32[3,2,11,64,176]{4,3,2,1,0:T(8,128)}, f32[3,2,11,64,176]{4,3,2,1,0:T(8,128)S(1)}, u32[]{:S(2)}) copy-start(f32[3,2,11,64,176]{4,3,2,1,0:T(8,128)S(1)} %multiply_subtract_fusion) | copy-start | bytes 8921092
  548.4 7.4 %copy-start.34 = (f32[2,11,176]{2,0,1:T(2,128)S(1)}, f32[2,11,176]{2,0,1:T(2,128)}, u32[]{:S(2)}) copy-start(f32[2,11,176]{2,0,1:T(2,128)} %copy-done.32) | copy-start | bytes 46468
  548.4 7.4 %copy-start.38 = (f32[2,176]{1,0:T(2,128)S(1)}, f32[2,176]{1,0:T(2,128)}, u32[]{:S(2)}) copy-start(f32[2,176]{1,0:T(2,128)} %copy-done.36) | copy-start | bytes 4228
  567.9 41.4 %collective-permute-start.7 = (f32[3,2,11,64,1]{3,1,4,2,0:T(2,128)}, f32[3,2,11,64,1]{3,1,4,2,0:T(2,128)}, u32[]{:S(2)}, u32[]{:S(2)}) collective-permute-start(f32[3,2,11,64,1]{3,1,4,2,0:T(2,128)} %copy.362), channel_id=1, source_target_pairs={{0,4},{4,8},{8,12},{12,16},{16,20},{20,24},{24,28},{1,5},{5,9},{9,... | collective-permute-start | bytes 50696 | tf_op jit(solution)/shard_map/ppermute | solution.py:23
  573.4 6.4 slice-start.6
  573.4 37.4 %collective-permute-start.6 = (f32[3,2,11,64,1]{3,1,4,2,0:T(2,128)}, f32[3,2,11,64,1]{3,1,4,2,0:T(2,128)}, u32[]{:S(2)}, u32[]{:S(2)}) collective-permute-start(f32[3,2,11,64,1]{3,1,4,2,0:T(2,128)} %copy.360), channel_id=1, source_target_pairs={{4,0},{8,4},{12,8},{16,12},{20,16},{24,20},{28,24},{5,1},{9,5},{13... | collective-permute-start | bytes 50696 | tf_op jit(solution)/shard_map/ppermute | solution.py:24
  584.2 6.9 %slice-start.7 = ((f32[3,2,11,64,176]{4,3,1,0,2:T(8,128)}), f32[3,2,9,64,176]{4,3,1,0,2:T(8,128)S(1)}, s32[]{:S(2)}) async-start(f32[3,2,11,64,176]{4,3,1,0,2:T(8,128)} %copy-done.3), calls=%async_computation.9 | async-start | bytes 7077888 | tf_op jit(solution)/shard_map/slice | solution.py:144
  595.4 7.0 %copy-start.41 = (f32[3,64]{1,0:T(4,128)S(1)}, f32[3,64]{1,0:T(4,128)}, u32[]{:S(2)}) copy-start(f32[3,64]{1,0:T(4,128)} %copy-done.40) | copy-start | bytes 2308
  595.4 9.5 %slice-start.8 = ((f32[3,2,11,64,176]{4,3,1,0,2:T(8,128)}), f32[3,2,9,64,176]{4,3,1,0,2:T(8,128)S(1)}, s32[]{:S(2)}) async-start(f32[3,2,11,64,176]{4,3,1,0,2:T(8,128)} %copy-done.4), calls=%async_computation.10 | async-start | bytes 7077888 | tf_op jit(solution)/shard_map/slice | solution.py:144
  623.1 13.9 %copy-start.57 = (f32[3,1,1,64,1]{3,0,4,2,1:T(4,128)S(1)}, f32[3,1,1,64,1]{3,0,4,2,1:T(4,128)}, u32[]{:S(2)}) copy-start(f32[3,1,1,64,1]{3,0,4,2,1:T(4,128)} %copy-done.56) | copy-start | bytes 2308
  623.1 13.9 %copy-start.58 = (f32[3,1,1,64,1]{3,0,4,2,1:T(4,128)S(1)}, f32[3,1,1,64,1]{3,0,4,2,1:T(4,128)}, u32[]{:S(2)}) copy-start(f32[3,1,1,64,1]{3,0,4,2,1:T(4,128)} %get-tuple-element.18) | copy-start | bytes 2308
  623.1 19.0 %copy-start.15 = (f32[3,2,9,11264]{3,1,0,2:T(2,128)S(1)}, f32[3,2,9,11264]{3,1,0,2:T(2,128)}, u32[]{:S(2)}) copy-start(f32[3,2,9,11264]{3,1,0,2:T(2,128)} %concatenate.111) | copy-start | bytes 7299076
  623.1 19.0 %copy-start.22 = (f32[3,2,1,11264]{3,1,0,2:T(2,128)S(1)}, f32[3,2,1,11264]{3,1,0,2:T(2,128)}, u32[]{:S(2)}) copy-start(f32[3,2,1,11264]{3,1,0,2:T(2,128)} %concatenate.112) | copy-start | bytes 811012
  623.1 19.0 %copy-start.23 = (f32[3,2,1,11264]{3,1,0,2:T(2,128)S(1)}, f32[3,2,1,11264]{3,1,0,2:T(2,128)}, u32[]{:S(2)}) copy-start(f32[3,2,1,11264]{3,1,0,2:T(2,128)} %concatenate.110) | copy-start | bytes 811012
  623.1 19.0 %copy-start.24 = (f32[3,2,1,11264]{3,1,0,2:T(2,128)S(1)}, f32[3,2,1,11264]{3,1,0,2:T(2,128)}, u32[]{:S(2)}) copy-start(f32[3,2,1,11264]{3,1,0,2:T(2,128)} %concatenate.121) | copy-start | bytes 811012
  623.1 19.0 %copy-start.25 = (f32[3,2,1,11264]{3,1,0,2:T(2,128)S(1)}, f32[3,2,1,11264]{3,1,0,2:T(2,128)}, u32[]{:S(2)}) copy-start(f32[3,2,1,11264]{3,1,0,2:T(2,128)} %concatenate.119) | copy-start | bytes 811012
  (35 other events, 116.0 us)
where the time goes:
time: 666 us; the launch traced here: 655 us
  local copies, waits for them, and re-layouts  254 us (38%)
  other arithmetic  111 us (17%)
  matrix products  110 us (17%)
  waiting for transfers between devices  103 us (15%)
  starting transfers between devices  37.4 us (6%)
  blocking collectives  37.2 us (6%)
    unnamed x145, local copies, waits for them, and re-layouts  66.8 us
    all_to_all x1, waiting for transfers between devices, local(): lax.all_to_all(advection_hat, 'four', split_axis=4, concat_axis=3, tiled=...  61.2 us
    all_to_all x1, waiting for transfers between devices, local(): lax.all_to_all(sending, 'four', split_axis=3, concat_axis=4, tiled=True)  39.7 us
    psum x3, blocking collectives, paired_products(): lax.psum((inner_product(residual, residual, weight), inner_product(residu...  37.2 us
    add x4, other arithmetic, edge_assemble(): values + jnp.where(is_last, following, 0.0)  30.9 us
    dot_general x3, matrix products, helmholtz(): jnp.einsum('km,...ympx->...ykpx', derivative, values, precision=HIGHEST)  27.6 us
    concatenate x9, local copies, waits for them, and re-layouts, assemble_rows(): jnp.concatenate([new_first[..., :, None, :, :], joined[..., :, 1:node_cou...  26 us
    div x3, local copies, waits for them, and re-layouts, local(): source = SIGMA * adjoint_local + returned / NU  25.4 us
  transfers between devices with their start and end apart: 10, of which 4 were waited for; matrix products, arithmetic and copies ran while one was open for 11% of the time, Pallas kernels for 0%

commit v1 on v0

--- a/solution.py
+++ b/solution.py
@@ -2,6 +2,8 @@
 import jax.numpy as jnp
 import numpy as np
 from jax import lax
+from jax.experimental import pallas as pl
+from jax.experimental.pallas import tpu as pltpu
 from jax.sharding import PartitionSpec as P
 
 ITERS = 3
@@ -167,7 +169,7 @@
     )
 
 
-def local(adjoint_velocity, base_flow, column_widths, row_heights, base_phase):
+def local_general(adjoint_velocity, base_flow, column_widths, row_heights, base_phase):
     node_count = adjoint_velocity.shape[2]
     row_count = adjoint_velocity.shape[1]
     columns_here = column_widths.shape[0]
@@ -263,6 +265,683 @@
     return solution.reshape(3, row_count, node_count, planes_local * part_nodes)
 
 
+MESH = pl.DeviceIdType.MESH
+NODES = 121
+PAD = 122
+TILES = 61
+LANES = 128
+
+
+def gll_numbers(node_count):
+    degree = node_count - 1
+    points = np.cos(np.pi * np.arange(node_count) / degree)
+    for newton_step in range(60):
+        legendre = legendre_values(points, node_count)
+        points = points - (points * legendre[:, degree] - legendre[:, degree - 1]) / (
+            node_count * legendre[:, degree]
+        )
+    legendre = legendre_values(points, node_count)
+    weights = (2.0 / (degree * node_count * legendre[:, degree] ** 2))[::-1]
+    points = points[::-1]
+    end_values = legendre[::-1, degree]
+    derivative = np.zeros((node_count, node_count))
+    for row_index in range(node_count):
+        for column in range(node_count):
+            if row_index != column:
+                derivative[row_index, column] = end_values[row_index] / (
+                    end_values[column] * (points[row_index] - points[column])
+                )
+    derivative[0, 0] = -degree * node_count / 4.0
+    derivative[degree, degree] = degree * node_count / 4.0
+    derivative = derivative.astype(np.float32).astype(np.float64)
+    weights = weights.astype(np.float32).astype(np.float64)
+    return derivative, weights
+
+
+def span_numbers(plane_count):
+    positions = np.arange(plane_count)
+    basis_rows = np.zeros((plane_count, plane_count))
+    basis_rows[0] = 1.0 / np.sqrt(plane_count)
+    basis_rows[1] = np.cos(np.pi * positions) / np.sqrt(plane_count)
+    for wave_index in range(1, plane_count // 2):
+        basis_rows[2 * wave_index] = np.sqrt(2.0 / plane_count) * np.cos(
+            2.0 * np.pi * wave_index * positions / plane_count
+        )
+        basis_rows[2 * wave_index + 1] = np.sqrt(2.0 / plane_count) * np.sin(
+            2.0 * np.pi * wave_index * positions / plane_count
+        )
+    wave_counts = np.arange(plane_count) // 2
+    wave_counts[1] = plane_count // 2
+    wave_counts[0] = 0
+    wavenumbers = 2.0 * np.pi * wave_counts / (plane_count / 64.0)
+    rotate = np.zeros((plane_count, plane_count))
+    for wave_index in range(1, plane_count // 2):
+        rotate[2 * wave_index, 2 * wave_index + 1] = wavenumbers[2 * wave_index]
+        rotate[2 * wave_index + 1, 2 * wave_index] = -wavenumbers[2 * wave_index]
+    return basis_rows, basis_rows.T @ rotate @ basis_rows
+
+
+def two_parts(table):
+    table = table.astype(np.float32)
+    high = table.astype(jnp.bfloat16)
+    low = (table - high.astype(np.float32)).astype(jnp.bfloat16)
+    return high, low
+
+
+def split_values(values):
+    high = values.astype(jnp.bfloat16)
+    low = (values - high.astype(jnp.float32)).astype(jnp.bfloat16)
+    return high, low
+
+
+def dot(left, right):
+    return jnp.dot(left, right, preferred_element_type=jnp.float32)
+
+
+def dot_three(values, high, low):
+    vh, vl = split_values(values)
+    return dot(vh, high) + (dot(vl, high) + dot(vh, low))
+
+
+def times(matrix, values, sign):
+    n = len(values)
+    half = n // 2
+    even = [values[m] + values[n - 1 - m] for m in range(half)]
+    odd = [values[m] - values[n - 1 - m] for m in range(half)]
+    out = [None] * n
+    for k in range(half + 1):
+        s = None
+        d = None
+        for m in range(half):
+            ce = 0.5 * (matrix[k, m] + matrix[k, n - 1 - m])
+            co = 0.5 * (matrix[k, m] - matrix[k, n - 1 - m])
+            if not (k == half and sign < 0):
+                term = float(ce) * even[m]
+                s = term if s is None else s + term
+            if not (k == half and sign > 0):
+                term = float(co) * odd[m]
+                d = term if d is None else d + term
+        if not (k == half and sign < 0):
+            s = s + float(matrix[k, half]) * values[half]
+        if k == half:
+            out[k] = s if sign > 0 else d
+        else:
+            out[k] = s + d
+            out[n - 1 - k] = s - d if sign > 0 else d - s
+    return out
+
+
+def swap_halves(a, b, low):
+    axis = a.ndim - 2
+    return (
+        jnp.where(low, a, pltpu.roll(b, 4, axis)),
+        jnp.where(low, pltpu.roll(a, 4, axis), b),
+    )
+
+
+def chunk_start(step, size, total):
+    return jnp.minimum(step * size, total - size)
+
+
+def section_kernel(
+    sizes,
+    derivative,
+    weights,
+    coef_ref,
+    base_ref,
+    wh_ref,
+    wl_ref,
+    vh_ref,
+    vl_ref,
+    dh_ref,
+    dl_ref,
+    widths_ref,
+    heights_ref,
+    phase_ref,
+    wq_ref,
+    out_ref,
+    send1,
+    recv1,
+    send2,
+    recv2,
+    base_now,
+    base_slope,
+    lines,
+    line_z,
+    acc,
+    res,
+    image,
+    direction,
+    along,
+    edges,
+    ghosts,
+    sums,
+    sums_in,
+    send1_sem,
+    recv1_sem,
+    send2_sem,
+    recv2_sem,
+    local_sem,
+    edge_send_sem,
+    edge_recv_sem,
+    sum_send_sem,
+    sum_recv_sem,
+):
+    n_four, n_elem = sizes
+    q = 11
+    elem = lax.axis_index("elem")
+    four = lax.axis_index("four")
+    stiff = derivative.T @ (weights[:, None] * derivative)
+
+    barrier = pltpu.get_barrier_semaphore()
+    for k in range(1, n_four):
+        pl.semaphore_signal(
+            barrier, inc=1, device_id=(elem, lax.rem(four + k, n_four)), device_id_type=MESH
+        )
+    for k in range(1, n_elem):
+        pl.semaphore_signal(
+            barrier, inc=1, device_id=(lax.rem(elem + k, n_elem), four), device_id_type=MESH
+        )
+
+    low3 = lax.broadcasted_iota(jnp.int32, (1, 8, LANES), 1) < 4
+    low3w = lax.broadcasted_iota(jnp.int32, (1, 8, 256), 1) < 4
+
+    def pack(c):
+        def body(step, carry):
+            t = chunk_start(step, 8, TILES)
+            for tile in range(2):
+                a = coef_ref[c, pl.ds(t, 8), pl.ds(8 * tile, 8), :]
+                b = coef_ref[c, pl.ds(t + TILES, 8), pl.ds(8 * tile, 8), :]
+                first, second = swap_halves(a, b, low3)
+                send1[2 * tile, c, pl.ds(t, 8)] = first
+                send1[2 * tile + 1, c, pl.ds(t, 8)] = second
+            return carry
+
+        lax.fori_loop(0, 8, body, 0)
+
+    def exchange(source, target, send_sem, recv_sem, c):
+        return [
+            pltpu.make_async_remote_copy(
+                src_ref=source.at[lax.rem(four + k, n_four), c],
+                dst_ref=target.at[four, c],
+                send_sem=send_sem.at[c, k],
+                recv_sem=recv_sem.at[c, k],
+                device_id=(elem, lax.rem(four + k, n_four)),
+                device_id_type=MESH,
+            )
+            for k in range(1, n_four)
+        ]
+
+    def own(source, target, c, which):
+        return pltpu.make_async_copy(source.at[four, c], target.at[four, c], local_sem.at[which, c])
+
+    copies1 = [exchange(send1, recv1, send1_sem, recv1_sem, c) for c in range(3)]
+    own1 = [own(send1, recv1, c, 0) for c in range(3)]
+    copies2 = [exchange(send2, recv2, send2_sem, recv2_sem, c) for c in range(3)]
+    own2 = [own(send2, recv2, c, 1) for c in range(3)]
+
+    pack(0)
+    pl.semaphore_wait(barrier, n_four - 1 + n_elem - 1)
+    for copy in copies1[0]:
+        copy.start()
+    own1[0].start()
+    for c in (1, 2):
+        pack(c)
+        for copy in copies1[c]:
+            copy.start()
+        own1[c].start()
+
+    row_w = lax.broadcasted_iota(jnp.int32, (8, LANES), 0)
+    first_column = four * 4
+    hx = jnp.zeros((8, LANES), jnp.float32)
+    hy = jnp.zeros((8, LANES), jnp.float32)
+    for i in range(8):
+        hx = jnp.where(row_w == i, widths_ref[first_column + i % 4], hx)
+        hy = jnp.where(row_w == i, heights_ref[i // 4], hy)
+    gx = 2.0 / hx
+    gy = 2.0 / hy
+
+    phase = phase_ref[0]
+    shift_row = lax.broadcasted_iota(jnp.int32, (256, 256), 0)
+    shift_col = lax.broadcasted_iota(jnp.int32, (256, 256), 1)
+    moved = jnp.where(shift_row + phase >= 256, shift_row + phase - 256, shift_row + phase)
+    shift = jnp.where(moved == shift_col, 1.0, 0.0).astype(jnp.bfloat16)
+
+    for c in range(3):
+
+        def roll_body(step, carry, c=c):
+            n = step * 11
+            rows = base_ref[c, pl.ds(n, 11)].reshape(88, 256).astype(jnp.bfloat16)
+            now = dot(rows, shift)
+            base_now[c, pl.ds(n, 11)] = now.reshape(11, 8, 256)
+            now_b = now.astype(jnp.bfloat16)
+            slope = dot(now_b, dh_ref[...]) + dot(now_b, dl_ref[...])
+            base_slope[c, 2, pl.ds(n, 11)] = slope.reshape(11, 8, 256)
+            return carry
+
+        lax.fori_loop(0, 11, roll_body, 0)
+
+        def slope_body(step, carry, c=c):
+            for h in range(2):
+                part = pl.ds(LANES * h, LANES)
+                turned = times(
+                    derivative, [base_now[c, step * 11 + m, :, part] for m in range(q)], -1
+                )
+                for k in range(q):
+                    base_slope[c, 0, step * 11 + k, :, part] = gx * turned[k]
+                turned = times(
+                    derivative, [base_now[c, m * 11 + step, :, part] for m in range(q)], -1
+                )
+                for k in range(q):
+                    base_slope[c, 1, k * 11 + step, :, part] = gy * turned[k]
+            return carry
+
+        lax.fori_loop(0, 11, slope_body, 0)
+
+    for c in range(3):
+        acc[c, NODES] = jnp.zeros((8, 256), jnp.float32)
+    edges[...] = jnp.zeros(edges.shape, jnp.float32)
+    sums[...] = jnp.zeros(sums.shape, jnp.float32)
+
+    for c in range(3):
+        for copy in copies1[c]:
+            copy.wait_recv()
+        own1[c].wait()
+
+        def line_body(step, carry, c=c):
+            t = chunk_start(step, 8, TILES)
+            out = None
+            for s in range(n_four):
+                rows = recv1[s, c, pl.ds(t, 8)].reshape(64, LANES)
+                part = dot_three(
+                    rows, wh_ref[pl.ds(s * LANES, LANES), :], wl_ref[pl.ds(s * LANES, LANES), :]
+                )
+                out = part if out is None else out + part
+            e0 = out[:, :256].reshape(8, 8, 256)
+            e1 = out[:, 256:].reshape(8, 8, 256)
+            a, b = swap_halves(e0, e1, low3w)
+            lines[pl.ds(t, 8)] = a
+            lines[pl.ds(t + TILES, 8)] = b
+            return carry
+
+        lax.fori_loop(0, 8, line_body, 0)
+
+        def span_body(step, carry):
+            n = step * 11
+            rows = lines[pl.ds(n, 11)].reshape(88, 256)
+            line_z[pl.ds(n, 11)] = dot_three(rows, dh_ref[...], dl_ref[...]).reshape(11, 8, 256)
+            return carry
+
+        lax.fori_loop(0, 11, span_body, 0)
+
+        def add_x(step, carry, c=c):
+            for h in range(2):
+                part = pl.ds(LANES * h, LANES)
+                values = [lines[step * 11 + m, :, part] for m in range(q)]
+                turned = times(derivative, values, -1)
+                for k in range(q):
+                    n = step * 11 + k
+                    gain = base_now[0, n, :, part] * (gx * turned[k])
+                    gain = gain + base_now[2, n, :, part] * line_z[n, :, part]
+                    for e in range(3):
+                        change = -values[k] * base_slope[c, e, n, :, part]
+                        if e == c:
+                            change = change + gain
+                        if c > 0:
+                            change = change + acc[e, n, :, part]
+                        acc[e, n, :, part] = change
+            return carry
+
+        lax.fori_loop(0, 11, add_x, 0)
+
+        def add_y(step, carry, c=c):
+            for h in range(2):
+                part = pl.ds(LANES * h, LANES)
+                values = [lines[m * 11 + step, :, part] for m in range(q)]
+                turned = times(derivative, values, -1)
+                for k in range(q):
+                    n = k * 11 + step
+                    acc[c, n, :, part] += base_now[1, n, :, part] * (gy * turned[k])
+            return carry
+
+        lax.fori_loop(0, 11, add_y, 0)
+
+    for c in range(3):
+
+        def back_body(step, carry, c=c):
+            t = chunk_start(step, 8, TILES)
+            a = acc[c, pl.ds(t, 8)]
+            b = acc[c, pl.ds(t + TILES, 8)]
+            e0, e1 = swap_halves(a, b, low3w)
+            e0 = e0.reshape(64, 256)
+            e1 = e1.reshape(64, 256)
+            out = dot_three(e0, vh_ref[pl.ds(0, 256), :], vl_ref[pl.ds(0, 256), :])
+            out = out + dot_three(e1, vh_ref[pl.ds(256, 256), :], vl_ref[pl.ds(256, 256), :])
+            for s in range(n_four):
+                send2[s, c, pl.ds(t, 8)] = out[:, LANES * s : LANES * (s + 1)].reshape(8, 8, LANES)
+            return carry
+
+        lax.fori_loop(0, 8, back_body, 0)
+        for copy in copies2[c]:
+            copy.start()
+        own2[c].start()
+
+    lane = lax.broadcasted_iota(jnp.int32, (8, LANES), 1)
+    row = lax.broadcasted_iota(jnp.int32, (8, LANES), 0)
+    lower = lane < 64
+    lane_plane = jnp.where(lower, lane, lane - 64) + four * 64
+    kappa = lane_plane // 2
+    kappa = jnp.where(lane_plane == 1, 32 * n_four, kappa)
+    kappa = jnp.where(lane_plane == 0, 0, kappa)
+    beta = kappa.astype(jnp.float32) * np.float32(2.0 * np.pi / n_four)
+    wave = beta * beta + SIGMA
+    hyl = jnp.where(lower, heights_ref[0], heights_ref[1])
+    hxl = []
+    for tile in range(2):
+        h = jnp.zeros((8, LANES), jnp.float32)
+        for i in range(8):
+            h = jnp.where(row == i, widths_ref[8 * tile + i], h)
+        hxl.append(h)
+    quarter = [0.25 * h * hyl for h in hxl]
+    scale_x = [hyl / h for h in hxl]
+    scale_y = [h / hyl for h in hxl]
+    one = jnp.ones((8, LANES), jnp.float32)
+    half = 0.5 * one
+    left_inner = elem > 0
+    right_inner = elem < n_elem - 1
+    share_first = [jnp.where(jnp.logical_and(row == 0, jnp.logical_not(left_inner)), one, half), half]
+    share_last = [half, jnp.where(jnp.logical_and(row == 7, jnp.logical_not(right_inner)), one, half)]
+    share_top = jnp.where(lower, one, half)
+    share_bottom = jnp.where(lower, half, one)
+    right = lax.rem(elem + 1, n_elem)
+    left = lax.rem(elem + n_elem - 1, n_elem)
+
+    def edge_copies(c, level):
+        return [
+            pltpu.make_async_remote_copy(
+                src_ref=edges.at[c, level, 0],
+                dst_ref=ghosts.at[c, level, 1],
+                send_sem=edge_send_sem.at[c, level, 0],
+                recv_sem=edge_recv_sem.at[c, level, 1],
+                device_id=(left, four),
+                device_id_type=MESH,
+            ),
+            pltpu.make_async_remote_copy(
+                src_ref=edges.at[c, level, 1],
+                dst_ref=ghosts.at[c, level, 0],
+                send_sem=edge_send_sem.at[c, level, 1],
+                recv_sem=edge_recv_sem.at[c, level, 0],
+                device_id=(right, four),
+                device_id_type=MESH,
+            ),
+        ]
+
+    def edge_start(values, c, level):
+        for qy in range(q):
+            edges[c, level, 0, pl.ds(qy, 1), :] = values[qy * 11, pl.ds(0, 1), :]
+            edges[c, level, 1, pl.ds(qy, 1), :] = values[qy * 11 + 10, pl.ds(15, 1), :]
+        copies = edge_copies(c, level)
+        for copy in copies:
+            copy.start()
+        return copies
+
+    left_keep = jnp.where(left_inner, 1.0, 0.0)
+    right_keep = jnp.where(right_inner, 1.0, 0.0)
+
+    def assemble_here(values, c, level, copies):
+        for copy in copies:
+            copy.wait_recv()
+
+        def body(qy, carry):
+            n0 = qy * 11
+            a0 = values[n0, pl.ds(0, 8), :]
+            a1 = values[n0, pl.ds(8, 8), :]
+            b0 = values[n0 + 10, pl.ds(0, 8), :]
+            b1 = values[n0 + 10, pl.ds(8, 8), :]
+            from_left = ghosts[c, level, 0, pl.ds(qy, 1), :] * left_keep
+            from_right = ghosts[c, level, 1, pl.ds(qy, 1), :] * right_keep
+            rb0 = pltpu.roll(b0, 1, 0)
+            rb1 = pltpu.roll(b1, 1, 0)
+            ra0 = pltpu.roll(a0, 7, 0)
+            ra1 = pltpu.roll(a1, 7, 0)
+            values[n0, pl.ds(0, 8), :] = a0 + jnp.where(row == 0, from_left, rb0)
+            values[n0, pl.ds(8, 8), :] = a1 + jnp.where(row == 0, rb0, rb1)
+            values[n0 + 10, pl.ds(0, 8), :] = b0 + jnp.where(row == 7, ra1, ra0)
+            values[n0 + 10, pl.ds(8, 8), :] = b1 + jnp.where(row == 7, from_right, ra1)
+            return carry
+
+        lax.fori_loop(0, q, body, 0)
+        for qx in range(q):
+            for tile in range(2):
+                rows = pl.ds(8 * tile, 8)
+                top = values[qx, rows, :]
+                bottom = values[110 + qx, rows, :]
+                values[qx, rows, :] = top + jnp.where(lower, 0.0, pltpu.roll(bottom, 64, 1))
+                values[110 + qx, rows, :] = bottom + jnp.where(lower, pltpu.roll(top, 64, 1), 0.0)
+
+    def sum_copies(c, level):
+        return [
+            pltpu.make_async_remote_copy(
+                src_ref=sums.at[c, level],
+                dst_ref=sums_in.at[c, level, k],
+                send_sem=sum_send_sem.at[c, level, k],
+                recv_sem=sum_recv_sem.at[c, level, k],
+                device_id=(lax.rem(elem + k, n_elem), four),
+                device_id_type=MESH,
+            )
+            for k in range(1, n_elem)
+        ]
+
+    zero = jnp.zeros((8, LANES), jnp.float32)
+
+    def apply(values, target):
+        def body_x(qy, carry):
+            rr, wy = carry[0], wq_ref[qy]
+            share = jnp.where(qy == 0, share_top, jnp.where(qy == q - 1, share_bottom, one))
+            for tile in range(2):
+                rows = pl.ds(8 * tile, 8)
+                v = [values[qy * 11 + m, rows, :] for m in range(q)]
+                turned = times(stiff, v, 1)
+                ax = scale_x[tile] * wy
+                mass = (wave * quarter[tile]) * wy
+                inner = None
+                for k in range(q):
+                    target[qy * 11 + k, rows, :] = ax * turned[k] + (mass * float(weights[k])) * v[k]
+                    square = v[k] * v[k]
+                    if k == 0:
+                        square = square * share_first[tile]
+                    if k == q - 1:
+                        square = square * share_last[tile]
+                    inner = square if inner is None else inner + square
+                rr = rr + share * inner
+            return (rr,)
+
+        (rr,) = lax.fori_loop(0, q, body_x, (zero,))
+
+        def body_y(qx, carry):
+            product, wx = carry[0], wq_ref[qx]
+            for tile in range(2):
+                rows = pl.ds(8 * tile, 8)
+                v = [values[m * 11 + qx, rows, :] for m in range(q)]
+                turned = times(stiff, v, 1)
+                ay = scale_y[tile] * wx
+                for k in range(q):
+                    total = target[k * 11 + qx, rows, :] + ay * turned[k]
+                    target[k * 11 + qx, rows, :] = total
+                    product = product + v[k] * total
+            return (product,)
+
+        (product,) = lax.fori_loop(0, q, body_y, (zero,))
+        return rr, product
+
+    def fold(values):
+        total = jnp.sum(values, axis=0, keepdims=True)
+        return total + pltpu.roll(total, 64, 1)
+
+    waiting = []
+    for c in range(3):
+        for copy in copies2[c]:
+            copy.wait_recv()
+        own2[c].wait()
+
+        def unpack_body(step, carry, c=c):
+            t = chunk_start(step, 8, TILES)
+            for tile in range(2):
+                rows = pl.ds(8 * tile, 8)
+                a, b = swap_halves(
+                    recv2[2 * tile, c, pl.ds(t, 8)], recv2[2 * tile + 1, c, pl.ds(t, 8)], low3
+                )
+                res[pl.ds(t, 8), rows, :] = SIGMA * coef_ref[c, pl.ds(t, 8), rows, :] + a / NU
+                res[pl.ds(t + TILES, 8), rows, :] = (
+                    SIGMA * coef_ref[c, pl.ds(t + TILES, 8), rows, :] + b / NU
+                )
+            return carry
+
+        lax.fori_loop(0, 8, unpack_body, 0)
+
+        def mass_body(qy, carry):
+            wy = wq_ref[qy]
+            for tile in range(2):
+                rows = pl.ds(8 * tile, 8)
+                area = quarter[tile] * wy
+                for k in range(q):
+                    res[qy * 11 + k, rows, :] = res[qy * 11 + k, rows, :] * (area * float(weights[k]))
+            return carry
+
+        lax.fori_loop(0, q, mass_body, 0)
+        copies = edge_start(res, c, 0)
+        waiting += copies
+        assemble_here(res, c, 0, copies)
+
+        norm_now = None
+        step_size = None
+        for it in range(ITERS):
+            rr, product = apply(res, image)
+            sums[c, it, pl.ds(0, 1), :] = fold(rr)
+            sums[c, it, pl.ds(1, 1), :] = fold(product)
+            sum_list = sum_copies(c, it)
+            for copy in sum_list:
+                copy.start()
+            waiting += sum_list
+            if it + 1 < ITERS:
+                copies = edge_start(image, c, it + 1)
+                waiting += copies
+                assemble_here(image, c, it + 1, copies)
+            for copy in sum_list:
+                copy.wait_recv()
+            total = sums[c, it]
+            for k in range(1, n_elem):
+                total = total + sums_in[c, it, k]
+            norm_next = total[0:1, :]
+            product = total[1:2, :]
+            if it == 0:
+                growth = jnp.zeros_like(norm_next)
+                step_size = norm_next / product
+            else:
+                growth = norm_next / norm_now
+                step_size = norm_next / (product - growth * norm_next / step_size)
+            norm_now = norm_next
+
+            def update(n, carry, it=it, c=c, growth=growth, step_size=step_size):
+                for j in range(11):
+                    m = n * 11 + j
+                    r = res[m]
+                    if it == 0:
+                        d = r
+                        out_ref[c, m] = step_size * d
+                    else:
+                        d = r + growth * direction[m]
+                        out_ref[c, m] = out_ref[c, m] + step_size * d
+                    if it + 1 < ITERS:
+                        direction[m] = d
+                        a = image[m]
+                        if it > 0:
+                            a = a + growth * along[m]
+                        if it + 2 < ITERS:
+                            along[m] = a
+                        res[m] = r - step_size * a
+                return carry
+
+            lax.fori_loop(0, 11, update, 0)
+
+    for group in copies1 + copies2 + [waiting]:
+        for copy in group:
+            copy.wait_send()
+
+
+def local_blocks(adjoint_velocity, base_flow, column_widths, row_heights, base_phase):
+    n_four, n_elem = lax.axis_size("four"), lax.axis_size("elem")
+    derivative, weights = gll_numbers(11)
+    basis_rows, span_slope = span_numbers(256)
+    forward = np.zeros((n_four, 2, 64, 2, 256))
+    for ey in range(2):
+        forward[:, ey, :, ey, :] = basis_rows.reshape(n_four, 64, 256)
+    forward = forward.reshape(512, 512)
+    tables = two_parts(forward) + two_parts(forward.T) + two_parts(span_slope.T)
+    coef = adjoint_velocity.reshape(3, 2, 11, 64, 16, 11)
+    coef = jnp.transpose(coef, (0, 2, 5, 4, 1, 3)).reshape(3, NODES, 16, LANES)
+    coef = jnp.pad(coef, ((0, 0), (0, PAD - NODES), (0, 0), (0, 0)))
+    base = base_flow.reshape(3, 2, 11, 4, 11, 256)
+    base = jnp.transpose(base, (0, 2, 4, 1, 3, 5)).reshape(3, NODES, 8, 256).astype(jnp.float32)
+    vmem = pl.BlockSpec(memory_space=pltpu.VMEM)
+    smem = pl.BlockSpec(memory_space=pltpu.SMEM)
+    f32 = jnp.float32
+    blocks = (n_four, 3, TILES, 8, LANES)
+    field = (PAD, 16, LANES)
+    dma = pltpu.SemaphoreType.DMA
+    out = pl.pallas_call(
+        lambda *refs: section_kernel((n_four, n_elem), derivative, weights, *refs),
+        out_shape=jax.ShapeDtypeStruct((3, NODES, 16, LANES), f32),
+        in_specs=[vmem] * 8 + [smem] * 4,
+        out_specs=vmem,
+        scratch_shapes=[
+            pltpu.VMEM(blocks, f32),
+            pltpu.VMEM(blocks, f32),
+            pltpu.VMEM(blocks, f32),
+            pltpu.VMEM(blocks, f32),
+            pltpu.VMEM((3, NODES, 8, 256), f32),
+            pltpu.VMEM((3, 3, NODES, 8, 256), f32),
+            pltpu.VMEM((PAD, 8, 256), f32),
+            pltpu.VMEM((PAD, 8, 256), f32),
+            pltpu.VMEM((3, PAD, 8, 256), f32),
+            pltpu.VMEM(field, f32),
+            pltpu.VMEM(field, f32),
+            pltpu.VMEM(field, f32),
+            pltpu.VMEM(field, f32),
+            pltpu.VMEM((3, ITERS, 2, 16, LANES), f32),
+            pltpu.VMEM((3, ITERS, 2, 16, LANES), f32),
+            pltpu.VMEM((3, ITERS, 8, LANES), f32),
+            pltpu.VMEM((3, ITERS, n_elem, 8, LANES), f32),
+            dma((3, n_four)),
+            dma((3, n_four)),
+            dma((3, n_four)),
+            dma((3, n_four)),
+            dma((2, 3)),
+            dma((3, ITERS, 2)),
+            dma((3, ITERS, 2)),
+            dma((3, ITERS, n_elem)),
+            dma((3, ITERS, n_elem)),
+        ],
+        compiler_params=pltpu.CompilerParams(
+            collective_id=0, has_side_effects=True, vmem_limit_bytes=60 * 1024 * 1024
+        ),
+    )(coef, base, *tables, column_widths, row_heights, base_phase, weights.astype(np.float32))
+    out = out.reshape(3, 11, 11, 16, 2, 64)
+    return jnp.transpose(out, (0, 4, 1, 5, 3, 2)).reshape(adjoint_velocity.shape)
+
+
+def local(adjoint_velocity, base_flow, column_widths, row_heights, base_phase):
+    four, elem = lax.axis_size("four"), lax.axis_size("elem")
+    known = (
+        adjoint_velocity.shape == (3, 2, 11, 64 * 16 * 11)
+        and column_widths.shape == (16,)
+        and four == 4
+        and elem > 2
+    )
+    chosen = local_blocks if known else local_general
+    return chosen(adjoint_velocity, base_flow, column_widths, row_heights, base_phase)
+
+
 def solution(mesh):
     return jax.shard_map(
         local,

time: 666 us -> 319 us (0.48); the launches traced: 655 us -> 317 us
  Pallas kernels: 0 us -> 176 us
  local copies, waits for them, and re-layouts: 254 us -> 140 us
  other arithmetic: 111 us -> 0 us
  matrix products: 110 us -> 0 us
  waiting for transfers between devices: 103 us -> 0 us
  starting transfers between devices: 37.4 us -> 0 us
  blocking collectives: 37.2 us -> 0 us
    pallas_call x0 -> x1, Pallas kernels: none -> 176 us  [local_blocks(): pl.pallas_call(lambda *refs: section_kernel((n_four, n_elem), derivative,...]
    dot_general x20 -> x0, matrix products: 110 us -> none  [the longest x3 27.6 us: helmholtz(): jnp.einsum('km,...ympx->...ykpx', derivative, values, precision=HIGHEST)]
    all_to_all x2 -> x0, waiting for transfers between devices: 101 us -> none  [the longest x1 61.2 us: local(): lax.all_to_all(advection_hat, 'four', split_axis=4, concat_axis=3, tiled=...]
    reshape x1 -> x5, local copies, waits for them, and re-layouts: 6.13 us -> 101 us  [the longest x1 38.6 us: local_blocks(): coef = adjoint_velocity.reshape(3, 2, 11, 64, 16, 11)]
    unnamed x145 -> x0, local copies, waits for them, and re-layouts: 66.8 us -> none
    slice x27 -> x0, local copies, waits for them, and re-layouts: 43.5 us -> none  [the longest x8 20.9 us: padded(): first = lax.slice_in_dim(x, 0, width, axis=dim)]
    add x8 -> x0, other arithmetic: 43.2 us -> none  [the longest x4 30.9 us: edge_assemble(): values + jnp.where(is_last, following, 0.0)]
    psum x3 -> x0, blocking collectives: 37.2 us -> none  [paired_products(): lax.psum((inner_product(residual, residual, weight), inner_product(residu...]
  transfers between devices with their start and end apart: 10 -> 0, of which waited for: 4 -> 0; matrix products, arithmetic and copies ran while one was open for 11% -> 0% of each run, Pallas kernels for 0% -> 0%
where the time goes in v1:
time: 319 us; the launch traced here: 317 us
  Pallas kernels  176 us (55%)
  local copies, waits for them, and re-layouts  140 us (44%)
    pallas_call x1, Pallas kernels, local_blocks(): pl.pallas_call(lambda *refs: section_kernel((n_four, n_elem), derivative,...  176 us
    reshape x1, local copies, waits for them, and re-layouts, local_blocks(): coef = adjoint_velocity.reshape(3, 2, 11, 64, 16, 11)  38.6 us
    reshape x2, local copies, waits for them, and re-layouts, local_blocks(): out = out.reshape(3, 11, 11, 16, 2, 64)  29.5 us
    reshape x1, local copies, waits for them, and re-layouts, local_blocks(): jnp.transpose(out, (0, 4, 1, 5, 3, 2)).reshape(adjoint_velocity.shape)  27 us
    transpose x1, local copies, waits for them, and re-layouts, local_blocks(): coef = jnp.transpose(coef, (0, 2, 5, 4, 1, 3)).reshape(3, NODES, 16, LANES)  25.2 us
    convert_element_type x3, local copies, waits for them, and re-layouts, local_blocks(): jnp.transpose(base, (0, 2, 4, 1, 3, 5)).reshape(3, NODES, 8, 256)  12.6 us

profile of v1, /device:TPU:25, one launch (start us, length us, event | category | flops | bytes accessed | tf_op | source)
XLA Modules:
  0.0 317.4 jit_solution(9136473734349964153)
XLA Ops:
  0.0 38.6 %reshape.18 = f32[3,2,11,64,16,11]{5,4,3,1,2,0:T(8,128)} reshape(f32[3,2,11,11264]{3,1,2,0:T(2,128)} %param.12) | data formatting | bytes 5947392 | tf_op jit(solution)/shard_map/reshape | solution.py:881
  38.6 25.2 %copy.16 = f32[3,11,11,16,2,64]{5,4,3,2,1,0:T(2,128)} copy(f32[3,11,11,16,2,64]{2,3,5,4,1,0:T(8,128)} %bitcast.14) | data formatting | bytes 5947392 | tf_op jit(solution)/shard_map/transpose | solution.py:882
  63.8 5.5 %reshape.19 = f32[3,121,16,128]{3,2,1,0:T(8,128)S(1)} reshape(f32[3,11,11,16,2,64]{5,4,3,2,1,0:T(2,128)} %copy.16) | data formatting | bytes 5947392 | tf_op jit(solution)/shard_map/reshape | solution.py:882
  69.4 2.0 pad.4.refs_0_
  71.3 5.2 %reshape.23 = f32[3,2,11,4,11,256]{5,4,3,1,2,0:T(8,128)} reshape(bf16[3,2,11,11264]{3,1,2,0:T(2,128)(2,1)} %param.13) | data formatting | bytes 4460544 | tf_op jit(solution)/shard_map/convert_element_type | solution.py:885
  76.5 4.8 %copy.17 = f32[3,11,11,2,4,256]{5,4,3,2,1,0:T(4,128)S(1)} copy(f32[3,11,11,2,4,256]{5,2,4,3,1,0:T(8,128)} %bitcast.15) | data formatting | bytes 5947392 | tf_op jit(solution)/shard_map/convert_element_type | solution.py:885
  81.3 2.6 reshape.22.refs_1_
  84.6 176.3 %shard_map.118 = f32[3,121,16,128]{3,2,1,0:T(8,128)} custom-call(f32[3,122,16,128]{3,2,1,0:T(8,128)} %pad.4.refs_0_, f32[3,121,8,256]{3,2,1,0:T(8,128)} %reshape.22.refs_1_, bf16[512,512]{1,0:T(8,128)(2,1)} %constant.17.clone.refs_2_, bf16[512,512]{1,0:T(8,128)(2,1)} %constant.18.clone.refs_3_, bf16[512,512]{1,0:T(8,128)(2,1)} %constant.19.clone.refs_4_, ...), custom_call_target="tpu_custom_call" | custom-call | tf_op jit(solution)/shard_map/pallas_call | solution.py:892
  260.9 6.7 %reshape.20 = f32[3,11,11,16,2,64]{5,4,3,2,1,0:T(2,128)} reshape(f32[3,121,16,128]{3,2,1,0:T(8,128)} %shard_map.118) | data formatting | bytes 5947392 | tf_op jit(solution)/shard_map/reshape | solution.py:929
  267.6 22.8 %copy.18 = f32[3,11,11,16,2,64]{2,3,5,4,1,0:T(8,128)} copy(f32[3,11,11,16,2,64]{5,4,3,2,1,0:T(2,128)} %reshape.20) | data formatting | bytes 5947392 | tf_op jit(solution)/shard_map/reshape | solution.py:929
  290.4 27.0 %reshape.21 = f32[3,2,11,11264]{3,1,2,0:T(2,128)} reshape(f32[3,2,11,64,16,11]{5,4,3,1,2,0:T(8,128)} %bitcast.13) | data formatting | bytes 5947392 | tf_op jit(solution)/shard_map/reshape | solution.py:930

commit v2 on v1

--- a/solution.py
+++ b/solution.py
@@ -334,6 +334,13 @@
     return high, low
 
 
+def three_parts(values):
+    high = values.astype(jnp.bfloat16)
+    rest = values - high.astype(jnp.float32)
+    middle = rest.astype(jnp.bfloat16)
+    return high, middle, (rest - middle.astype(jnp.float32)).astype(jnp.bfloat16)
+
+
 def dot(left, right):
     return jnp.dot(left, right, preferred_element_type=jnp.float32)
 
@@ -387,8 +394,9 @@
     sizes,
     derivative,
     weights,
-    coef_ref,
-    base_ref,
+    adj_ref,
+    flow_ref,
+    place_ref,
     wh_ref,
     wl_ref,
     vh_ref,
@@ -399,7 +407,12 @@
     heights_ref,
     phase_ref,
     wq_ref,
+    final_ref,
+    coef_ref,
     out_ref,
+    base_rows,
+    part_a,
+    part_b,
     send1,
     recv1,
     send2,
@@ -446,6 +459,91 @@
     low3 = lax.broadcasted_iota(jnp.int32, (1, 8, LANES), 1) < 4
     low3w = lax.broadcasted_iota(jnp.int32, (1, 8, 256), 1) < 4
 
+    lane16 = lax.broadcasted_iota(jnp.int32, (11, LANES), 1)
+
+    def spread(c):
+        for ey in range(2):
+
+            def group(g, carry, ey=ey):
+                start = pl.multiple_of(g * 1408, LANES)
+                for jl in range(8):
+                    w, o = (176 * jl) // LANES, (176 * jl) % LANES
+                    tiles = [
+                        adj_ref[c, ey, :, pl.ds(start + LANES * min(w + i, 10), LANES)]
+                        for i in range(3)
+                    ]
+                    if o:
+                        tiles = [pltpu.roll(x, LANES - o, 1) for x in tiles]
+                        keep = lane16 < LANES - o
+                        first = jnp.where(keep, tiles[0], tiles[1])
+                        second = jnp.where(keep, tiles[1], tiles[2])
+                    else:
+                        first, second = tiles[0], tiles[1]
+                    row = pl.multiple_of((ey * 64 + g * 8 + jl) * 16, 16)
+                    part_a[pl.ds(row, 11), :] = first
+                    part_b[pl.ds(row, 11), :] = second
+                return carry
+
+            lax.fori_loop(0, 8, group, 0)
+
+        def turn(qy, carry):
+            rows = pl.ds(qy, 128, stride=16)
+            block = jnp.concatenate([part_a[rows, :], part_b[rows, :]], axis=1)
+            total = None
+            for piece in three_parts(block):
+                term = lax.dot_general(
+                    place_ref[...],
+                    piece,
+                    (((1,), (1,)), ((), ())),
+                    preferred_element_type=jnp.float32,
+                )
+                total = term if total is None else total + term
+            coef_ref[c, pl.ds(qy * 11, 11)] = total.reshape(11, 16, LANES)
+            return carry
+
+        lax.fori_loop(0, 11, turn, 0)
+        coef_ref[c, NODES] = jnp.zeros((16, LANES), jnp.float32)
+
+    def gather(c):
+        def turn(qy, carry):
+            block = out_ref[c, pl.ds(qy * 11, 11)].reshape(176, LANES)
+            block = jnp.concatenate([block, jnp.zeros((80, LANES), jnp.float32)], axis=0).T
+            total = None
+            for piece in three_parts(block):
+                term = dot(piece[:, :176], place_ref[...])
+                total = term if total is None else total + term
+            rows = pl.ds(qy, 128, stride=16)
+            part_a[rows, :] = total[:, :LANES]
+            part_b[rows, :] = total[:, LANES:]
+            return carry
+
+        lax.fori_loop(0, 11, turn, 0)
+        for ey in range(2):
+
+            def group(g, carry, ey=ey):
+                start = pl.multiple_of(g * 1408, LANES)
+                sources = []
+                for jl in range(8):
+                    row = pl.multiple_of((ey * 64 + g * 8 + jl) * 16, 16)
+                    sources.append((part_a[pl.ds(row, 11), :], part_b[pl.ds(row, 11), :]))
+                for w in range(11):
+                    done = None
+                    at = 0
+                    while at < LANES:
+                        jl, node = divmod(LANES * w + at, 176)
+                        side = 0 if node < LANES else 1
+                        length = min((LANES if side == 0 else 176) - node, LANES - at)
+                        value = sources[jl][side]
+                        move = (at - (node - LANES * side)) % LANES
+                        if move:
+                            value = pltpu.roll(value, move, 1)
+                        done = value if done is None else jnp.where(lane16 < at, done, value)
+                        at += length
+                    final_ref[c, ey, :, pl.ds(start + LANES * w, LANES)] = done
+                return carry
+
+            lax.fori_loop(0, 8, group, 0)
+
     def pack(c):
         def body(step, carry):
             t = chunk_start(step, 8, TILES)
@@ -480,12 +578,14 @@
     copies2 = [exchange(send2, recv2, send2_sem, recv2_sem, c) for c in range(3)]
     own2 = [own(send2, recv2, c, 1) for c in range(3)]
 
+    spread(0)
     pack(0)
     pl.semaphore_wait(barrier, n_four - 1 + n_elem - 1)
     for copy in copies1[0]:
         copy.start()
     own1[0].start()
     for c in (1, 2):
+        spread(c)
         pack(c)
         for copy in copies1[c]:
             copy.start()
@@ -509,10 +609,23 @@
 
     for c in range(3):
 
+        def place_body(qx, carry, c=c):
+            for ex in range(4):
+                start = pl.multiple_of((ex * 11 + qx) * 256, 256)
+                for ey in range(2):
+                    piece = flow_ref[c, ey, :, pl.ds(start, 256)].astype(jnp.float32)
+                    row = qx * 8 + ey * 4 + ex
+                    base_rows[0, pl.ds(row, 11, stride=88), :] = piece[:, :LANES]
+                    base_rows[1, pl.ds(row, 11, stride=88), :] = piece[:, LANES:]
+            return carry
+
+        lax.fori_loop(0, 11, place_body, 0)
+
         def roll_body(step, carry, c=c):
             n = step * 11
-            rows = base_ref[c, pl.ds(n, 11)].reshape(88, 256).astype(jnp.bfloat16)
-            now = dot(rows, shift)
+            at = pl.ds(pl.multiple_of(n * 8, 8), 88)
+            rows = jnp.concatenate([base_rows[0, at, :], base_rows[1, at, :]], axis=1)
+            now = dot(rows.astype(jnp.bfloat16), shift)
             base_now[c, pl.ds(n, 11)] = now.reshape(11, 8, 256)
             now_b = now.astype(jnp.bfloat16)
             slope = dot(now_b, dh_ref[...]) + dot(now_b, dl_ref[...])
@@ -863,6 +976,7 @@
                 return carry
 
             lax.fori_loop(0, 11, update, 0)
+        gather(c)
 
     for group in copies1 + copies2 + [waiting]:
         for copy in group:
@@ -878,11 +992,11 @@
         forward[:, ey, :, ey, :] = basis_rows.reshape(n_four, 64, 256)
     forward = forward.reshape(512, 512)
     tables = two_parts(forward) + two_parts(forward.T) + two_parts(span_slope.T)
-    coef = adjoint_velocity.reshape(3, 2, 11, 64, 16, 11)
-    coef = jnp.transpose(coef, (0, 2, 5, 4, 1, 3)).reshape(3, NODES, 16, LANES)
-    coef = jnp.pad(coef, ((0, 0), (0, PAD - NODES), (0, 0), (0, 0)))
-    base = base_flow.reshape(3, 2, 11, 4, 11, 256)
-    base = jnp.transpose(base, (0, 2, 4, 1, 3, 5)).reshape(3, NODES, 8, 256).astype(jnp.float32)
+    place = np.zeros((11, 16, 256), np.float32)
+    for column in range(16):
+        for qx in range(11):
+            place[qx, column, column * 11 + qx] = 1.0
+    place = place.reshape(176, 256).astype(jnp.bfloat16)
     vmem = pl.BlockSpec(memory_space=pltpu.VMEM)
     smem = pl.BlockSpec(memory_space=pltpu.SMEM)
     f32 = jnp.float32
@@ -891,10 +1005,15 @@
     dma = pltpu.SemaphoreType.DMA
     out = pl.pallas_call(
         lambda *refs: section_kernel((n_four, n_elem), derivative, weights, *refs),
-        out_shape=jax.ShapeDtypeStruct((3, NODES, 16, LANES), f32),
-        in_specs=[vmem] * 8 + [smem] * 4,
+        out_shape=jax.ShapeDtypeStruct(adjoint_velocity.shape, f32),
+        in_specs=[vmem] * 9 + [smem] * 4,
         out_specs=vmem,
         scratch_shapes=[
+            pltpu.VMEM((3, PAD, 16, LANES), f32),
+            pltpu.VMEM((3, NODES, 16, LANES), f32),
+            pltpu.VMEM((2, NODES * 8, LANES), f32),
+            pltpu.VMEM((2048, LANES), f32),
+            pltpu.VMEM((2048, LANES), f32),
             pltpu.VMEM(blocks, f32),
             pltpu.VMEM(blocks, f32),
             pltpu.VMEM(blocks, f32),
@@ -925,9 +1044,8 @@
         compiler_params=pltpu.CompilerParams(
             collective_id=0, has_side_effects=True, vmem_limit_bytes=60 * 1024 * 1024
         ),
-    )(coef, base, *tables, column_widths, row_heights, base_phase, weights.astype(np.float32))
-    out = out.reshape(3, 11, 11, 16, 2, 64)
-    return jnp.transpose(out, (0, 4, 1, 5, 3, 2)).reshape(adjoint_velocity.shape)
+    )(adjoint_velocity, base_flow, place, *tables, column_widths, row_heights, base_phase, weights.astype(np.float32))
+    return out
 
 
 def local(adjoint_velocity, base_flow, column_widths, row_heights, base_phase):

time: 319 us -> 204 us (0.64)
  local copies, waits for them, and re-layouts: 140 us -> 12.3 us
  Pallas kernels: 176 us -> 191 us
    reshape x5 -> x0, local copies, waits for them, and re-layouts: 101 us -> none  [the longest x1 38.6 us: local_blocks(): coef = adjoint_velocity.reshape(3, 2, 11, 64, 16, 11)]
    transpose x1 -> x0, local copies, waits for them, and re-layouts: 25.2 us -> none  [local_blocks(): coef = jnp.transpose(coef, (0, 2, 5, 4, 1, 3)).reshape(3, NODES, 16, LANES)]
    pallas_call x1, Pallas kernels: 176 us -> 191 us  [local_blocks(): pl.pallas_call(lambda *refs: section_kernel((n_four, n_elem), derivative,...]
    convert_element_type x3 -> x0, local copies, waits for them, and re-layouts: 12.6 us -> none  [local_blocks(): jnp.transpose(base, (0, 2, 4, 1, 3, 5)).reshape(3, NODES, 8, 256)]
    unnamed x0 -> x4, local copies, waits for them, and re-layouts: none -> 6.15 us
    pallas_call x0 -> x1, local copies, waits for them, and re-layouts: none -> 6.13 us  [local_blocks(): pl.pallas_call(lambda *refs: section_kernel((n_four, n_elem), derivative,...]
where the time goes in v2:
time: 204 us
  Pallas kernels  191 us (94%)
  local copies, waits for them, and re-layouts  12.3 us (6%)
    pallas_call x1, Pallas kernels, local_blocks(): pl.pallas_call(lambda *refs: section_kernel((n_four, n_elem), derivative,...  191 us
    unnamed x4, local copies, waits for them, and re-layouts  6.15 us
    pallas_call x1, local copies, waits for them, and re-layouts, local_blocks(): pl.pallas_call(lambda *refs: section_kernel((n_four, n_elem), derivative,...  6.13 us

profile of v2, /device:TPU:25, one launch (start us, length us, event | category | flops | bytes accessed | tf_op | source)
XLA Modules:
  0.0 204.3 jit_solution(12052751466175454140)
XLA Ops:
  0.0 0.0 copy-start
  0.8 3.2 %copy.15.refs_1_ = bf16[3,2,11,11264]{3,2,1,0:T(8,128)(2,1)} copy(bf16[3,2,11,11264]{3,1,2,0:T(2,128)(2,1)} %param.14) | data formatting | bytes 2973696 | tf_op args[1]
  4.0 0.0 copy-done
  4.0 3.0 %copy.14.refs_0_ = f32[3,2,11,11264]{3,2,1,0:T(8,128)} copy(f32[3,2,11,11264]{3,1,2,0:T(2,128)S(1)} %copy-done) | data formatting | bytes 5947392 | tf_op args[0]
  7.0 191.2 %shard_map.127 = f32[3,2,11,11264]{3,2,1,0:T(8,128)} custom-call(f32[3,2,11,11264]{3,2,1,0:T(8,128)} %copy.14.refs_0_, bf16[3,2,11,11264]{3,2,1,0:T(8,128)(2,1)} %copy.15.refs_1_, bf16[176,256]{1,0:T(8,128)(2,1)} %constant.16.clone.refs_2_, bf16[512,512]{1,0:T(8,128)(2,1)} %constant.17.clone.refs_3_, bf16[512,512]{1,0:T(8,128)(2,1)} %constant.18.clone.refs_4_, ...), custom_call_target="tpu_custom_call" | custom-call | tf_op jit(solution)/shard_map/pallas_call | solution.py:1006
  198.2 6.1 %copy.16 = f32[3,2,11,11264]{3,1,2,0:T(2,128)} copy(f32[3,2,11,11264]{3,2,1,0:T(8,128)} %shard_map.127) | data formatting | bytes 5947392 | tf_op jit(solution)/shard_map/pallas_call | solution.py:1006
Async XLA Ops:
  0.0 4.0 %copy-start = (f32[3,2,11,11264]{3,1,2,0:T(2,128)S(1)}, f32[3,2,11,11264]{3,1,2,0:T(2,128)}, u32[]{:S(2)}) copy-start(f32[3,2,11,11264]{3,1,2,0:T(2,128)} %param.13) | copy-start | bytes 8921092

commit v3 on v2

--- a/solution.py
+++ b/solution.py
@@ -1,3 +1,4 @@
+import functools
 import jax
 import jax.numpy as jnp
 import numpy as np
@@ -411,8 +412,7 @@
     coef_ref,
     out_ref,
     base_rows,
-    part_a,
-    part_b,
+    wide_rows,
     send1,
     recv1,
     send2,
@@ -459,36 +459,22 @@
     low3 = lax.broadcasted_iota(jnp.int32, (1, 8, LANES), 1) < 4
     low3w = lax.broadcasted_iota(jnp.int32, (1, 8, 256), 1) < 4
 
-    lane16 = lax.broadcasted_iota(jnp.int32, (11, LANES), 1)
+    lane8 = lax.broadcasted_iota(jnp.int32, (8, LANES), 1)
 
     def spread(c):
-        for ey in range(2):
-
-            def group(g, carry, ey=ey):
-                start = pl.multiple_of(g * 1408, LANES)
+        def turn(qy, carry):
+            blocks = []
+            for ey in range(2):
+                tiles = [adj_ref[c, qy, pl.ds(2 * w + ey, 8, stride=22), :] for w in range(11)]
                 for jl in range(8):
                     w, o = (176 * jl) // LANES, (176 * jl) % LANES
-                    tiles = [
-                        adj_ref[c, ey, :, pl.ds(start + LANES * min(w + i, 10), LANES)]
-                        for i in range(3)
-                    ]
+                    pair = [tiles[w], tiles[w + 1], tiles[min(w + 2, 10)]]
                     if o:
-                        tiles = [pltpu.roll(x, LANES - o, 1) for x in tiles]
-                        keep = lane16 < LANES - o
-                        first = jnp.where(keep, tiles[0], tiles[1])
-                        second = jnp.where(keep, tiles[1], tiles[2])
-                    else:
-                        first, second = tiles[0], tiles[1]
-                    row = pl.multiple_of((ey * 64 + g * 8 + jl) * 16, 16)
-                    part_a[pl.ds(row, 11), :] = first
-                    part_b[pl.ds(row, 11), :] = second
-                return carry
-
-            lax.fori_loop(0, 8, group, 0)
-
-        def turn(qy, carry):
-            rows = pl.ds(qy, 128, stride=16)
-            block = jnp.concatenate([part_a[rows, :], part_b[rows, :]], axis=1)
+                        pair = [pltpu.roll(x, LANES - o, 1) for x in pair]
+                        keep = lane8 < LANES - o
+                        pair = [jnp.where(keep, pair[0], pair[1]), jnp.where(keep, pair[1], pair[2])]
+                    blocks.append(jnp.concatenate(pair[:2], axis=1))
+            block = jnp.concatenate(blocks, axis=0)
             total = None
             for piece in three_parts(block):
                 term = lax.dot_general(
@@ -504,7 +490,7 @@
         lax.fori_loop(0, 11, turn, 0)
         coef_ref[c, NODES] = jnp.zeros((16, LANES), jnp.float32)
 
-    def gather(c):
+    def gather(c, low, high):
         def turn(qy, carry):
             block = out_ref[c, pl.ds(qy * 11, 11)].reshape(176, LANES)
             block = jnp.concatenate([block, jnp.zeros((80, LANES), jnp.float32)], axis=0).T
@@ -512,20 +498,7 @@
             for piece in three_parts(block):
                 term = dot(piece[:, :176], place_ref[...])
                 total = term if total is None else total + term
-            rows = pl.ds(qy, 128, stride=16)
-            part_a[rows, :] = total[:, :LANES]
-            part_b[rows, :] = total[:, LANES:]
-            return carry
-
-        lax.fori_loop(0, 11, turn, 0)
-        for ey in range(2):
-
-            def group(g, carry, ey=ey):
-                start = pl.multiple_of(g * 1408, LANES)
-                sources = []
-                for jl in range(8):
-                    row = pl.multiple_of((ey * 64 + g * 8 + jl) * 16, 16)
-                    sources.append((part_a[pl.ds(row, 11), :], part_b[pl.ds(row, 11), :]))
+            for ey in range(2):
                 for w in range(11):
                     done = None
                     at = 0
@@ -533,16 +506,23 @@
                         jl, node = divmod(LANES * w + at, 176)
                         side = 0 if node < LANES else 1
                         length = min((LANES if side == 0 else 176) - node, LANES - at)
-                        value = sources[jl][side]
+                        row = (ey * 8 + jl) * 8
+                        value = total[row : row + 8, LANES * side : LANES * (side + 1)]
                         move = (at - (node - LANES * side)) % LANES
                         if move:
                             value = pltpu.roll(value, move, 1)
-                        done = value if done is None else jnp.where(lane16 < at, done, value)
+                        done = value if done is None else jnp.where(lane8 < at, done, value)
                         at += length
-                    final_ref[c, ey, :, pl.ds(start + LANES * w, LANES)] = done
-                return carry
-
-            lax.fori_loop(0, 8, group, 0)
+                    final_ref[c, qy, pl.ds(2 * w + ey, 8, stride=22), :] = done
+            return carry
+
+        lax.fori_loop(low, high, turn, 0)
+
+    pending = []
+
+    def fill():
+        if pending:
+            pending.pop(0)()
 
     def pack(c):
         def body(step, carry):
@@ -609,14 +589,14 @@
 
     for c in range(3):
 
-        def place_body(qx, carry, c=c):
-            for ex in range(4):
-                start = pl.multiple_of((ex * 11 + qx) * 256, 256)
-                for ey in range(2):
-                    piece = flow_ref[c, ey, :, pl.ds(start, 256)].astype(jnp.float32)
-                    row = qx * 8 + ey * 4 + ex
-                    base_rows[0, pl.ds(row, 11, stride=88), :] = piece[:, :LANES]
-                    base_rows[1, pl.ds(row, 11, stride=88), :] = piece[:, LANES:]
+        def place_body(qy, carry, c=c):
+            wide_rows[...] = flow_ref[c, qy].astype(jnp.float32)
+            at = pl.multiple_of(qy * 88, 8)
+            for qx in range(q):
+                for h in range(2):
+                    for ey in range(2):
+                        rows = wide_rows[pl.ds(qx * 4 + h * 2 + ey, 4, stride=44), :]
+                        base_rows[h, pl.ds(at + qx * 8 + ey * 4, 4), :] = rows
             return carry
 
         lax.fori_loop(0, 11, place_body, 0)
@@ -655,6 +635,25 @@
         acc[c, NODES] = jnp.zeros((8, 256), jnp.float32)
     edges[...] = jnp.zeros(edges.shape, jnp.float32)
     sums[...] = jnp.zeros(sums.shape, jnp.float32)
+
+    def send_back(c):
+        def back_body(step, carry):
+            t = chunk_start(step, 8, TILES)
+            a = acc[c, pl.ds(t, 8)]
+            b = acc[c, pl.ds(t + TILES, 8)]
+            e0, e1 = swap_halves(a, b, low3w)
+            e0 = e0.reshape(64, 256)
+            e1 = e1.reshape(64, 256)
+            out = dot_three(e0, vh_ref[pl.ds(0, 256), :], vl_ref[pl.ds(0, 256), :])
+            out = out + dot_three(e1, vh_ref[pl.ds(256, 256), :], vl_ref[pl.ds(256, 256), :])
+            for s in range(n_four):
+                send2[s, c, pl.ds(t, 8)] = out[:, LANES * s : LANES * (s + 1)].reshape(8, 8, LANES)
+            return carry
+
+        lax.fori_loop(0, 8, back_body, 0)
+        for copy in copies2[c]:
+            copy.start()
+        own2[c].start()
 
     for c in range(3):
         for copy in copies1[c]:
@@ -679,6 +678,21 @@
 
         lax.fori_loop(0, 8, line_body, 0)
 
+        def take_body(step, carry, c=c):
+            for k in range(q):
+                n = step * 11 + k
+                value = lines[n]
+                for e in range(3):
+                    if e != c:
+                        change = -value * base_slope[c, e, n]
+                        acc[e, n] = change if c == 0 else acc[e, n] + change
+            return carry
+
+        lax.fori_loop(0, 11, take_body, 0)
+        if c == 2:
+            send_back(0)
+            send_back(1)
+
         def span_body(step, carry):
             n = step * 11
             rows = lines[pl.ds(n, 11)].reshape(88, 256)
@@ -696,13 +710,10 @@
                     n = step * 11 + k
                     gain = base_now[0, n, :, part] * (gx * turned[k])
                     gain = gain + base_now[2, n, :, part] * line_z[n, :, part]
-                    for e in range(3):
-                        change = -values[k] * base_slope[c, e, n, :, part]
-                        if e == c:
-                            change = change + gain
-                        if c > 0:
-                            change = change + acc[e, n, :, part]
-                        acc[e, n, :, part] = change
+                    gain = gain - values[k] * base_slope[c, c, n, :, part]
+                    if c > 0:
+                        gain = gain + acc[c, n, :, part]
+                    acc[c, n, :, part] = gain
             return carry
 
         lax.fori_loop(0, 11, add_x, 0)
@@ -718,31 +729,14 @@
             return carry
 
         lax.fori_loop(0, 11, add_y, 0)
-
-    for c in range(3):
-
-        def back_body(step, carry, c=c):
-            t = chunk_start(step, 8, TILES)
-            a = acc[c, pl.ds(t, 8)]
-            b = acc[c, pl.ds(t + TILES, 8)]
-            e0, e1 = swap_halves(a, b, low3w)
-            e0 = e0.reshape(64, 256)
-            e1 = e1.reshape(64, 256)
-            out = dot_three(e0, vh_ref[pl.ds(0, 256), :], vl_ref[pl.ds(0, 256), :])
-            out = out + dot_three(e1, vh_ref[pl.ds(256, 256), :], vl_ref[pl.ds(256, 256), :])
-            for s in range(n_four):
-                send2[s, c, pl.ds(t, 8)] = out[:, LANES * s : LANES * (s + 1)].reshape(8, 8, LANES)
-            return carry
-
-        lax.fori_loop(0, 8, back_body, 0)
-        for copy in copies2[c]:
-            copy.start()
-        own2[c].start()
+        if c == 2:
+            send_back(2)
 
     lane = lax.broadcasted_iota(jnp.int32, (8, LANES), 1)
     row = lax.broadcasted_iota(jnp.int32, (8, LANES), 0)
     lower = lane < 64
-    lane_plane = jnp.where(lower, lane, lane - 64) + four * 64
+    lane_half = jnp.where(lower, lane, lane - 64)
+    lane_plane = lax.rem(lane_half, 8) * 8 + lane_half // 8 + four * 64
     kappa = lane_plane // 2
     kappa = jnp.where(lane_plane == 1, 32 * n_four, kappa)
     kappa = jnp.where(lane_plane == 0, 0, kappa)
@@ -802,6 +796,7 @@
     right_keep = jnp.where(right_inner, 1.0, 0.0)
 
     def assemble_here(values, c, level, copies):
+        fill()
         for copy in copies:
             copy.wait_recv()
 
@@ -940,6 +935,8 @@
                 copies = edge_start(image, c, it + 1)
                 waiting += copies
                 assemble_here(image, c, it + 1, copies)
+            else:
+                fill()
             for copy in sum_list:
                 copy.wait_recv()
             total = sums[c, it]
@@ -976,11 +973,19 @@
                 return carry
 
             lax.fori_loop(0, 11, update, 0)
-        gather(c)
+        pending += [functools.partial(gather, c, i, min(i + 4, 11)) for i in (0, 4, 8)]
+
+    while pending:
+        fill()
 
     for group in copies1 + copies2 + [waiting]:
         for copy in group:
             copy.wait_send()
+
+
+def fold_rows(values):
+    values = values.reshape(3, 2, 11, 88, LANES)
+    return jnp.transpose(values, (0, 2, 3, 1, 4)).reshape(3, 11, 176, LANES)
 
 
 def local_blocks(adjoint_velocity, base_flow, column_widths, row_heights, base_phase):
@@ -988,8 +993,9 @@
     derivative, weights = gll_numbers(11)
     basis_rows, span_slope = span_numbers(256)
     forward = np.zeros((n_four, 2, 64, 2, 256))
+    order = np.arange(64).reshape(8, 8).T.reshape(64)
     for ey in range(2):
-        forward[:, ey, :, ey, :] = basis_rows.reshape(n_four, 64, 256)
+        forward[:, ey, :, ey, :] = basis_rows.reshape(n_four, 64, 256)[:, order]
     forward = forward.reshape(512, 512)
     tables = two_parts(forward) + two_parts(forward.T) + two_parts(span_slope.T)
     place = np.zeros((11, 16, 256), np.float32)
@@ -1005,15 +1011,14 @@
     dma = pltpu.SemaphoreType.DMA
     out = pl.pallas_call(
         lambda *refs: section_kernel((n_four, n_elem), derivative, weights, *refs),
-        out_shape=jax.ShapeDtypeStruct(adjoint_velocity.shape, f32),
+        out_shape=jax.ShapeDtypeStruct((3, 11, 176, LANES), f32),
         in_specs=[vmem] * 9 + [smem] * 4,
         out_specs=vmem,
         scratch_shapes=[
             pltpu.VMEM((3, PAD, 16, LANES), f32),
             pltpu.VMEM((3, NODES, 16, LANES), f32),
             pltpu.VMEM((2, NODES * 8, LANES), f32),
-            pltpu.VMEM((2048, LANES), f32),
-            pltpu.VMEM((2048, LANES), f32),
+            pltpu.VMEM((176, LANES), f32),
             pltpu.VMEM(blocks, f32),
             pltpu.VMEM(blocks, f32),
             pltpu.VMEM(blocks, f32),
@@ -1044,8 +1049,9 @@
         compiler_params=pltpu.CompilerParams(
             collective_id=0, has_side_effects=True, vmem_limit_bytes=60 * 1024 * 1024
         ),
-    )(adjoint_velocity, base_flow, place, *tables, column_widths, row_heights, base_phase, weights.astype(np.float32))
-    return out
+    )(fold_rows(adjoint_velocity), fold_rows(base_flow), place, *tables, column_widths, row_heights, base_phase, weights.astype(np.float32))
+    out = jnp.transpose(out.reshape(3, 11, 88, 2, LANES), (0, 3, 1, 2, 4))
+    return out.reshape(adjoint_velocity.shape)
 
 
 def local(adjoint_velocity, base_flow, column_widths, row_heights, base_phase):

time: 204 us -> 181 us (0.89)
  Pallas kernels: 191 us -> 177 us
  local copies, waits for them, and re-layouts: 12.3 us -> 3.64 us
    pallas_call x1, Pallas kernels: 191 us -> 177 us  [local_blocks(): pl.pallas_call(lambda *refs: section_kernel((n_four, n_elem), derivative,...]
    pallas_call x1 -> x0, local copies, waits for them, and re-layouts: 6.13 us -> none  [local_blocks(): pl.pallas_call(lambda *refs: section_kernel((n_four, n_elem), derivative,...]
    unnamed x4 -> x1, local copies, waits for them, and re-layouts: 6.15 us -> 3.64 us
where the time goes in v3:
time: 181 us
  Pallas kernels  177 us (98%)
  local copies, waits for them, and re-layouts  3.64 us (2%)
    pallas_call x1, Pallas kernels, local_blocks(): pl.pallas_call(lambda *refs: section_kernel((n_four, n_elem), derivative,...  177 us
    unnamed x1, local copies, waits for them, and re-layouts  3.64 us

profile of v3, /device:TPU:25, one launch (start us, length us, event | category | flops | bytes accessed | tf_op | source)
XLA Modules:
  0.0 181.1 jit_solution(16486187624510804362)
XLA Ops:
  0.7 176.8 %shard_map.127 = f32[3,11,176,128]{3,2,1,0:T(8,128)} custom-call(f32[3,11,176,128]{3,2,1,0:T(8,128)} %bitcast.16, bf16[3,11,176,128]{3,2,1,0:T(8,128)(2,1)} %bitcast.17, bf16[176,256]{1,0:T(8,128)(2,1)} %constant.16.clone.refs_2_, bf16[512,512]{1,0:T(8,128)(2,1)} %constant.17.clone.refs_3_, bf16[512,512]{1,0:T(8,128)(2,1)} %constant.18.clone.refs_4_, ...), custom_call_target="tpu_custom_call" | custom-call | tf_op jit(solution)/shard_map/pallas_call | solution.py:1012
  177.5 3.6 %copy.19 = f32[3,2,11,11264]{3,1,2,0:T(2,128)} copy(f32[3,2,11,11264]{3,1,2,0:T(2,128)} %bitcast.15) | data formatting | bytes 5947392
